TPU v7x, 256 devices: a whole 4x4x8 slice. The times are simulated.
256 devices in a mesh: leaf: 256 (over x, z, y, core).
Axes of the slice: x: 4, y: 4, z: 8, core: 2. Of those that a mesh axis runs over, the one named last changes fastest.
Arguments:
- rhs: float32 [16, 1048576], P(None, 'leaf'), may hold values from -6 to 6
- order: int32 [256, 4096], P('leaf'), may hold values from 0 to 4095, each once within a row
- leaf_basis: float32 [16384, 4096], P('leaf'), may hold values from -0.75 to 0.75
- near_pick: int32 [3, 16384], P(None, 'leaf'), may hold values from -1 to 1
- near_block: float32 [3, 16384, 4096], P(None, 'leaf'), may hold values from -0.4375 to 0.4375
- trans_one: float32 [16384, 4096], P('leaf'), may hold values from -0.5 to 0.5
- trans_two: float32 [8192, 4096], P('leaf'), may hold values from -0.5 to 0.5
- trans_root: float32 [4096, 4096], P('leaf'), may hold values from -0.1875 to 0.1875
- far_pick_a: int32 [3, 16384], P(None, 'leaf'), may hold values from 0 to 3
- far_block_a: float32 [3, 16384, 4096], P(None, 'leaf'), may hold values from -0.4375 to 0.4375
- far_pick_b: int32 [3, 8192], P(None, 'leaf'), may hold values from 0 to 3
- far_block_b: float32 [3, 8192, 4096], P(None, 'leaf'), may hold values from -0.4375 to 0.4375
- far_pick_c: int32 [3, 4096], P(None, 'leaf'), may hold values from 0 to 3
- far_block_c: float32 [3, 4096, 4096], P(None, 'leaf'), may hold values from -0.4375 to 0.4375
- top_transfer: float32 [3, 256, 4096], P(None, 'leaf'), may hold values from -1 to 1, as said below
- top_source: int32 [1024], P('leaf'), may hold values from 0 to 31
- top_target: int32 [1024], P('leaf'), may hold values from 0 to 31
- top_block: float32 [1024, 4096], P('leaf'), may hold values from -0.75 to 0.75
Outputs:
- product_out: float32 [16, 1048576], P(None, 'leaf')
Inputs may be any that keep to these rules, and one draw needn't show every extreme that they name: `top_transfer`: entry [j, d] equals entry [j, d - d % 2^j].
All inputs are finite; a program needn't handle non-finite values.
Results may differ from a plain program's by a relative error of at most 0.0001.
Values sent between devices are 32-bit elements; how exact they have to be, the bound alone decides.
A program may use at most 128 MiB of HBM per device.

v0:
```python
import jax
import jax.numpy as jnp
from jax import lax
from jax.sharding import PartitionSpec as P

LEAF = 64
RANK = 64


exactly = lax.Precision.HIGHEST


def with_halo(value, sides, width):
    for axis, dim in sides:
        count, length = (lax.axis_size(axis), value.shape[dim])
        up = [(i, (i + 1) % count) for i in range(count - 1)]
        down = [(j, i) for i, j in up]
        last = lax.slice_in_dim(value, length - width, length, axis=dim)
        initial = lax.slice_in_dim(value, 0, width, axis=dim)
        before = lax.ppermute(last, axis, up)
        after = lax.ppermute(initial, axis, down)
        value = jnp.concatenate([before, value, after], axis=dim)
    return value


def from_partner(value, axis, apart):
    mask = 2**apart
    pairs = [(source, source ^ mask) for source in range(lax.axis_size(axis))]
    return lax.ppermute(value, axis, pairs)


def product(form, first, second):
    return jnp.einsum(form, first, second, precision=exactly)


def square(flat, rows_count, cols_count):
    return flat.reshape(flat.shape[:-1] + (rows_count, cols_count))


def ascend(transfer, coeffs):
    carried = product("njk,jrn->krn", square(transfer, RANK, RANK), coeffs)
    return carried.reshape(coeffs.shape[0], coeffs.shape[1], -1, 2).sum(-1)


def descend(transfer, parents, fanout):
    return product(
        "nkj,jrn->krn", square(transfer, RANK, RANK), jnp.repeat(parents, fanout, axis=2)
    )


def far_product(picks, blocks, padded, node_count):
    offsets = jnp.where(picks < 2, picks - 3, picks)
    result = jnp.zeros((padded.shape[0], padded.shape[1], node_count), jnp.float32)
    for which_slot in range(picks.shape[0]):
        indices = jnp.arange(node_count, dtype=jnp.int32) + offsets[which_slot] + 3
        source = jnp.take(padded, indices, axis=2)
        result = result + product("nkj,jrn->krn", square(blocks[which_slot], RANK, RANK), source)
    return result


def body(
    rhs,
    order,
    leaf_basis,
    near_pick,
    near_block,
    trans_one,
    trans_two,
    trans_root,
    far_pick_a,
    far_block_a,
    far_pick_b,
    far_block_b,
    far_pick_c,
    far_block_c,
    top_transfer,
    top_source,
    top_target,
    top_block,
):
    columns, per_device = rhs.shape
    leaves = leaf_basis.shape[0]
    basis = square(leaf_basis, LEAF, RANK)
    ordered = jnp.take(rhs, order[0], axis=1).reshape(columns, leaves, LEAF)
    level_zero = product("npk,rnp->krn", basis, ordered)
    level_one = ascend(trans_one, level_zero)
    level_two = ascend(trans_two, level_one)
    levels = (level_two, level_one, level_zero)
    padded_levels = []
    for coeffs in levels:
        padded_levels.append(with_halo(coeffs, (("leaf", 2),), 3))
    padded_rows = with_halo(ordered, (("leaf", 1),), 1)
    root_mats = square(trans_root, RANK, RANK)
    rooted = product("njk,jrn->kr", root_mats, level_two)
    top_count = top_transfer.shape[0]
    group_size = 2**top_count
    devices = lax.axis_size("leaf")
    myself = lax.axis_index("leaf")
    top_nodes = devices // group_size
    climbing = jnp.dot(square(top_transfer[0, 0], RANK, RANK).T, rooted, precision=exactly)
    summed = climbing
    for height in range(top_count):
        summed = climbing + from_partner(climbing, "leaf", height)
        if height + 1 < top_count:
            climbing = jnp.dot(
                square(top_transfer[height + 1, 0], RANK, RANK).T, summed, precision=exactly
            )
    offered = summed * (1.0 / group_size)
    selector = (jnp.arange(top_nodes) == myself // group_size).astype(jnp.float32)
    everyone = lax.all_gather(offered[:, :, None], "leaf", axis=2, tiled=True)
    top_coeffs = everyone.reshape(RANK, columns, top_nodes, group_size).sum(-1)
    source_hot = (jnp.arange(top_nodes)[:, None] == top_source[None, :]).astype(jnp.float32)
    target_hot = (jnp.arange(top_nodes)[:, None] == top_target[None, :]).astype(jnp.float32)
    picked = product("krt,tb->krb", top_coeffs, source_hot)
    coupled = product("bkj,jrb->krb", square(top_block, RANK, RANK), picked)
    spread = product("krb,tb->krt", coupled, target_hot)
    falling_all = lax.psum(spread, "leaf")
    falling = product("krt,t->kr", falling_all, selector)
    for height in range(top_count - 1, -1, -1):
        falling = jnp.dot(square(top_transfer[height, 0], RANK, RANK), falling, precision=exactly)
    down_two = far_product(far_pick_c, far_block_c, padded_levels[0], leaves // 4) + product(
        "nkj,jr->krn", root_mats, falling
    )
    down_one = far_product(far_pick_b, far_block_b, padded_levels[1], leaves // 2) + descend(
        trans_two, down_two, 2
    )
    down_zero = far_product(far_pick_a, far_block_a, padded_levels[2], leaves) + descend(
        trans_one, down_one, 2
    )
    values = product("npk,krn->rnp", basis, down_zero)
    for which_slot in range(near_pick.shape[0]):
        indices = jnp.arange(leaves, dtype=jnp.int32) + near_pick[which_slot] + 1
        source = jnp.take(padded_rows, indices, axis=1)
        values = values + product(
            "npq,rnq->rnp", square(near_block[which_slot], LEAF, LEAF), source
        )
    flat_values = values.reshape(columns, per_device)
    return jnp.zeros((columns, per_device), jnp.float32).at[:, order[0]].set(flat_values)


def solution(mesh):
    in_specs = (
        P(None, "leaf"),
        P("leaf", None),
        P("leaf", None),
        P(None, "leaf"),
        P(None, "leaf", None),
        P("leaf", None),
        P("leaf", None),
        P("leaf", None),
        P(None, "leaf"),
        P(None, "leaf", None),
        P(None, "leaf"),
        P(None, "leaf", None),
        P(None, "leaf"),
        P(None, "leaf", None),
        P(None, "leaf", None),
        P("leaf"),
        P("leaf"),
        P("leaf", None),
    )
    out_specs = P(None, "leaf")
    return jax.shard_map(body, mesh=mesh, in_specs=in_specs, out_specs=out_specs, check_vma=False)
```

profile of v0, /device:TPU:1, one launch (start us, length us, event | category | flops | bytes accessed | tf_op | source)
XLA Modules:
  0.0 549.9 jit_solution(18156433651899625818)
XLA Ops:
  7.3 1.5 copy.28
  8.9 14.1 %gather_fusion = f32[4096,16]{1,0:T(8,128)} fusion(f32[16,4096]{0,1:T(8,128)S(1)} %copy.28, s32[4096]{0:T(1024)S(1)} %broadcast_clamp_fusion), kind=kCustom, calls=%fused_computation.12 | custom fusion | bytes 540672 | tf_op jit(solution)/shard_map/jit(_take)/gather | solution.py:84
  23.0 2.2 copy.29
  26.4 2.0 reshape.98
  29.3 1.9 convolution_bitcast_fusion
  31.9 5.1 collective-permute-start.1
  37.0 1.9 collective-permute-start
  39.0 3.1 reshape.99
  42.1 3.5 bitcast_reduce_fusion.1
  46.3 3.0 collective-permute-start.3
  49.3 1.5 reshape.101
  51.7 1.5 slice_reduce_fusion.2
  53.2 1.9 reshape.103
  56.6 1.4 convolution_bitcast_fusion.7
  58.0 1.5 convolution_bitcast_fusion.6
  60.8 2.4 collective-permute-start.10
  63.9 3.7 fusion.89
  72.7 1.6 fusion.88
  79.2 1.5 convolution_bitcast_fusion.5
  82.3 3.1 reshape_squeeze.48
  85.4 3.2 reshape_squeeze.49
  88.6 3.1 reshape_squeeze.50
  91.7 2.4 reshape_squeeze.51
  94.1 2.5 reshape_squeeze.52
  96.5 2.4 reshape_squeeze.53
  99.0 2.0 reshape_squeeze.54
  101.0 2.0 reshape_squeeze.55
  104.0 1.6 reshape.105
  106.4 3.2 reshape_squeeze.60
  109.6 2.2 reshape_squeeze.61
  111.8 3.2 reshape_squeeze.62
  115.0 2.9 collective-permute-start.9
  118.7 1.9 collective-permute-start.5
  120.7 3.6 collective-permute-start.8
  125.0 1.5 gather_fusion.10
  126.6 1.7 gather_fusion.11
  128.3 1.6 gather_fusion.12
  129.8 2.8 collective-permute-start.4
  133.3 6.0 %collective-permute-start.2 = (f32[64,16,3]{0,1,2:T(8,128)}, f32[64,16,3]{0,1,2:T(8,128)S(1)}, u32[]{:S(2)}, u32[]{:S(2)}) collective-permute-start(f32[64,16,3]{0,1,2:T(8,128)} %get-tuple-element.52), channel_id=1, source_target_pairs={{0,1},{1,2},{2,3},{3,4},{4,5},{5,6},{6,7},{7,8},{8,9},{9,10},{10,1... | collective-permute-start | bytes 36872 | tf_op jit(solution)/shard_map/ppermute | solution.py:20
  140.0 2.7 fusion.43
  143.5 1.6 gather_fusion.1
  145.1 1.6 gather_fusion.2
  146.7 1.6 gather_fusion.3
  150.7 1.5 gather_fusion.5
  154.6 2.8 convolution_add_fusion.10
  157.4 3.1 fusion.22
  160.6 3.2 convolution_add_fusion.8
  163.8 2.5 convolution_add_fusion.7
  166.3 3.4 fusion.12
  169.8 3.4 convolution_add_fusion.5
  173.2 4.6 convolution_add_fusion.4
  177.9 71.3 %all-gather.2.cloned.1.call-done = f32[64,16,256]{0,1,2:T(8,128)} async-done(((f32[64,16,1]{0,1,2:T(8,128)}), f32[64,16,256]{0,1,2:T(8,128)}) %all-gather.2.cloned.1.call-update) | async-done | bytes 1048592 | tf_op jit(solution)/shard_map/all_gather | solution.py:110
  249.1 1.8 bitcast_reduce_fusion
  252.7 2.7 fusion.4
  255.4 246.7 %all-reduce.2.cloned.1.call-done = f32[64,16,32]{0,2,1:T(8,128)} async-done(((f32[64,16,32]{0,2,1:T(8,128)}), f32[64,16,32]{0,2,1:T(8,128)}) %all-reduce.2.cloned.1.call-update) | async-done | bytes 131088 | tf_op jit(solution)/shard_map/psum | solution.py:117
  506.2 2.4 fusion.3
  508.7 1.7 fusion.2
  510.5 3.4 fusion.1
  513.9 3.4 fusion.98
  517.3 3.6 convolution_add_fusion.2
  520.9 3.4 convolution_add_fusion.1
  524.4 3.4 fusion
  528.2 2.0 copy.34
  530.2 11.4 %scatter_custom_fusion = f32[16,4096]{0,1:T(8,128)S(1)} fusion(s32[4096]{0:T(1024)S(1)} %bitcast.199, f32[4096,16]{1,0:T(8,128)} %copy.34, f32[]{:T(128)} %constant.48.clone.1), kind=kCustom, calls=%fused_computation.39 | custom fusion | bytes 262656 | tf_op jit(solution)/shard_map/scatter | solution.py:138
  (175 shorter events, 38.1 us)
Async XLA Ops:
  6.5 242.6 %all-gather.2.cloned.1.call-start = ((), (), s32[]{:S(2)}) async-start(), calls=%async_computation | async-start | bytes 2105344 | tf_op jit(solution)/shard_map/all_gather | solution.py:110
  8.8 16.8 %copy-start.30 = (s32[1,4096]{1,0:T(1,128)S(1)}, s32[1,4096]{1,0:T(1,128)}, u32[]{:S(2)}) copy-start(s32[1,4096]{1,0:T(1,128)} %param.27) | copy-start | bytes 49156
  28.5 0.8 copy-start.11
  31.2 14.3 %copy-start.9 = (f32[64,16,64]{0,1,2:T(8,128)}, f32[64,16,64]{0,1,2:T(8,128)S(1)}, u32[]{:S(2)}) copy-start(f32[64,16,64]{0,1,2:T(8,128)S(1)} %convolution_bitcast_fusion) | copy-start | bytes 786436
  31.9 110.8 %collective-permute-start.1 = (f32[64,16,3]{0,1,2:T(8,128)}, f32[64,16,3]{0,1,2:T(8,128)}, u32[]{:S(2)}, u32[]{:S(2)}) collective-permute-start(f32[64,16,3]{0,1,2:T(8,128)} %get-tuple-element.51), channel_id=1, source_target_pairs={{1,0},{2,1},{3,2},{4,3},{5,4},{6,5},{7,6},{8,7},{9,8},{10,9},{11,1... | collective-permute-start | bytes 36872 | tf_op jit(solution)/shard_map/ppermute | solution.py:21
  37.0 105.7 %collective-permute-start = (f32[64,16,3]{0,1,2:T(8,128)}, f32[64,16,3]{0,1,2:T(8,128)}, u32[]{:S(2)}, u32[]{:S(2)}) collective-permute-start(f32[64,16,3]{0,1,2:T(8,128)} %get-tuple-element.50), channel_id=1, source_target_pairs={{0,1},{1,2},{2,3},{3,4},{4,5},{5,6},{6,7},{7,8},{8,9},{9,10},{10,1... | collective-permute-start | bytes 36872 | tf_op jit(solution)/shard_map/ppermute | solution.py:20
  45.6 12.4 %copy-start.15 = (f32[64,16,32]{0,1,2:T(8,128)}, f32[64,16,32]{0,1,2:T(8,128)S(1)}, u32[]{:S(2)}) copy-start(f32[64,16,32]{0,1,2:T(8,128)S(1)} %bitcast_reduce_fusion.1) | copy-start | bytes 393220
  46.3 102.0 %collective-permute-start.3 = (f32[64,16,3]{0,1,2:T(8,128)}, f32[64,16,3]{0,1,2:T(8,128)}, u32[]{:S(2)}, u32[]{:S(2)}) collective-permute-start(f32[64,16,3]{0,1,2:T(8,128)} %get-tuple-element.53), channel_id=1, source_target_pairs={{1,0},{2,1},{3,2},{4,3},{5,4},{6,5},{7,6},{8,7},{9,8},{10,9},{11,1... | collective-permute-start | bytes 36872 | tf_op jit(solution)/shard_map/ppermute | solution.py:21
  50.7 16.9 %copy-start.1 = (f32[32,64,64]{2,1,0:T(8,128)}, f32[32,64,64]{2,1,0:T(8,128)S(1)}, u32[]{:S(2)}) copy-start(f32[32,64,64]{2,1,0:T(8,128)S(1)} %reshape.101) | copy-start | bytes 1572868
  59.5 19.7 %collective-permute-start.6 = (f32[64,16]{0,1:T(8,128)}, f32[64,16]{0,1:T(8,128)}, u32[]{:S(2)}, u32[]{:S(2)}) collective-permute-start(f32[64,16]{0,1:T(8,128)} %convolution_bitcast_fusion.6), channel_id=1, source_target_pairs={{0,1},{1,0},{2,3},{3,2},{4,5},{5,4},{6,7},{7,6},{8,9},{9,8},{10,11... | collective-permute-start | bytes 12296 | tf_op jit(solution)/shard_map/ppermute | solution.py:29
  60.8 57.9 %collective-permute-start.10 = (f32[16,1,64]{2,0,1:T(8,128)}, f32[16,1,64]{2,0,1:T(8,128)}, u32[]{:S(2)}, u32[]{:S(2)}) collective-permute-start(f32[16,1,64]{2,0,1:T(8,128)} %get-tuple-element.49), channel_id=1, source_target_pairs={{1,0},{2,1},{3,2},{4,3},{5,4},{6,5},{7,6},{8,7},{9,8},{10,9},{11,1... | collective-permute-start | bytes 12296 | tf_op jit(solution)/shard_map/ppermute | solution.py:21
  63.9 3.8 copy-start.36
  63.9 5.0 copy-start.24
  67.6 2.4 copy-start.37
  67.6 3.6 copy-start.26
  68.8 3.2 copy-start.38
  68.8 3.8 copy-start.14
  72.7 1.6 copy-start.48
  80.7 34.2 %collective-permute-start.7 = (f32[64,16]{0,1:T(8,128)}, f32[64,16]{0,1:T(8,128)}, u32[]{:S(2)}, u32[]{:S(2)}) collective-permute-start(f32[64,16]{0,1:T(8,128)} %convolution_bitcast_fusion.5), channel_id=1, source_target_pairs={{0,2},{1,3},{2,0},{3,1},{4,6},{5,7},{6,4},{7,5},{8,10},{9,11},{10,... | collective-permute-start | bytes 12296 | tf_op jit(solution)/shard_map/ppermute | solution.py:29
  106.4 11.4 %copy-start.29 = (f32[64,64]{1,0:T(8,128)}, f32[64,64]{1,0:T(8,128)S(1)}, u32[]{:S(2)}) copy-start(f32[64,64]{1,0:T(8,128)S(1)} %reshape_squeeze.59) | copy-start | bytes 49156
  111.8 3.2 copy-start.33
  111.8 7.0 %copy-start.32 = (f32[64,16,3]{0,1,2:T(8,128)S(1)}, f32[64,16,3]{0,1,2:T(8,128)}, u32[]{:S(2)}) copy-start(f32[64,16,3]{0,1,2:T(8,128)} %get-tuple-element.55) | copy-start | bytes 36868
  111.8 12.5 %copy-start.12 = (f32[16,64,64]{2,0,1:T(8,128)S(1)}, f32[16,64,64]{2,0,1:T(8,128)}, u32[]{:S(2)}) copy-start(f32[16,64,64]{2,0,1:T(8,128)} %copy-done.11) | copy-start | bytes 786436
  115.0 5.7 %collective-permute-start.9 = (f32[16,1,64]{2,0,1:T(8,128)S(1)}, f32[16,1,64]{2,0,1:T(8,128)S(1)}, u32[]{:S(2)}, u32[]{:S(2)}) collective-permute-start(f32[16,1,64]{2,0,1:T(8,128)S(1)} %copy-done.33), channel_id=1, source_target_pairs={{0,1},{1,2},{2,3},{3,4},{4,5},{5,6},{6,7},{7,8},{8,9},{9,10},{10,1... | collective-permute-start | bytes 12296 | tf_op jit(solution)/shard_map/ppermute | solution.py:20
  118.7 11.1 %copy-start.31 = (f32[64,16,3]{0,1,2:T(8,128)S(1)}, f32[64,16,3]{0,1,2:T(8,128)}, u32[]{:S(2)}) copy-start(f32[64,16,3]{0,1,2:T(8,128)} %get-tuple-element.54) | copy-start | bytes 36868
  118.7 14.6 %collective-permute-start.5 = (f32[64,16,3]{0,1,2:T(8,128)S(1)}, f32[64,16,3]{0,1,2:T(8,128)S(1)}, u32[]{:S(2)}, u32[]{:S(2)}) collective-permute-start(f32[64,16,3]{0,1,2:T(8,128)S(1)} %copy-done.32), channel_id=1, source_target_pairs={{1,0},{2,1},{3,2},{4,3},{5,4},{6,5},{7,6},{8,7},{9,8},{10,9},{11,1... | collective-permute-start | bytes 36872 | tf_op jit(solution)/shard_map/ppermute | solution.py:21
  120.7 9.1 %collective-permute-start.8 = (f32[64,16]{0,1:T(8,128)S(1)}, f32[64,16]{0,1:T(8,128)S(1)}, u32[]{:S(2)}, u32[]{:S(2)}) collective-permute-start(f32[64,16]{0,1:T(8,128)S(1)} %convolution_bitcast_fusion.4), channel_id=1, source_target_pairs={{0,4},{1,5},{2,6},{3,7},{4,0},{5,1},{6,2},{7,3},{8,12},{9,13},{10,... | collective-permute-start | bytes 12296 | tf_op jit(solution)/shard_map/ppermute | solution.py:29
  125.0 15.0 %copy-start.39 = (pred[16]{0:T(512)(128)(4,1)S(1)}, pred[16]{0:T(512)(128)(4,1)}, u32[]{:S(2)}) copy-start(pred[16]{0:T(512)(128)(4,1)} %get-tuple-element.62) | copy-start | bytes 52
  126.6 16.2 %copy-start.10 = (f32[64,16,64]{0,1,2:T(8,128)S(1)}, f32[64,16,64]{0,1,2:T(8,128)}, u32[]{:S(2)}) copy-start(f32[64,16,64]{0,1,2:T(8,128)} %copy-done.9) | copy-start | bytes 786436
  129.8 9.5 %collective-permute-start.4 = (f32[64,16,3]{0,1,2:T(8,128)S(1)}, f32[64,16,3]{0,1,2:T(8,128)S(1)}, u32[]{:S(2)}, u32[]{:S(2)}) collective-permute-start(f32[64,16,3]{0,1,2:T(8,128)S(1)} %copy-done.31), channel_id=1, source_target_pairs={{0,1},{1,2},{2,3},{3,4},{4,5},{5,6},{6,7},{7,8},{8,9},{9,10},{10,1... | collective-permute-start | bytes 36872 | tf_op jit(solution)/shard_map/ppermute | solution.py:20
  133.3 368.9 %all-reduce.2.cloned.1.call-start = ((), (), s32[]{:S(2)}) async-start(), calls=%async_computation.1 | async-start | bytes 524288 | tf_op jit(solution)/shard_map/psum | solution.py:117
  133.3 14.9 %collective-permute-start.2 = (f32[64,16,3]{0,1,2:T(8,128)}, f32[64,16,3]{0,1,2:T(8,128)S(1)}, u32[]{:S(2)}, u32[]{:S(2)}) collective-permute-start(f32[64,16,3]{0,1,2:T(8,128)} %get-tuple-element.52), channel_id=1, source_target_pairs={{0,1},{1,2},{2,3},{3,4},{4,5},{5,6},{6,7},{7,8},{8,9},{9,10},{10,1... | collective-permute-start | bytes 36872 | tf_op jit(solution)/shard_map/ppermute | solution.py:20
  150.7 3.9 copy-start.28
  150.7 3.9 copy-start.35
  152.2 5.2 copy-start.34
  153.1 7.5 %copy-start.16 = (f32[32,64,16]{1,2,0:T(8,128)S(1)}, f32[32,64,16]{1,2,0:T(8,128)}, u32[]{:S(2)}) copy-start(f32[32,64,16]{1,2,0:T(8,128)} %gather_fusion.5) | copy-start | bytes 393220
  153.1 7.5 %copy-start.42 = (pred[32]{0:T(512)(128)(4,1)S(1)}, pred[32]{0:T(512)(128)(4,1)}, u32[]{:S(2)}) copy-start(pred[32]{0:T(512)(128)(4,1)} %get-tuple-element.64) | copy-start | bytes 100
  154.6 9.1 %copy-start.13 = (f32[32,64,64]{2,1,0:T(8,128)S(1)}, f32[32,64,64]{2,1,0:T(8,128)}, u32[]{:S(2)}) copy-start(f32[32,64,64]{2,1,0:T(8,128)} %reshape_squeeze.53) | copy-start | bytes 1572868
  154.6 9.1 %copy-start.41 = (pred[32]{0:T(512)(128)(4,1)S(1)}, pred[32]{0:T(512)(128)(4,1)}, u32[]{:S(2)}) copy-start(pred[32]{0:T(512)(128)(4,1)} %get-tuple-element.24) | copy-start | bytes 100
  160.5 5.8 %copy-start.8 = (f32[64,64,64]{2,1,0:T(8,128)S(1)}, f32[64,64,64]{2,1,0:T(8,128)}, u32[]{:S(2)}) copy-start(f32[64,64,64]{2,1,0:T(8,128)} %reshape_squeeze.48) | copy-start | bytes 3145732
  160.5 5.8 %copy-start.23 = (f32[64,64,16]{1,2,0:T(8,128)S(1)}, f32[64,64,16]{1,2,0:T(8,128)}, u32[]{:S(2)}) copy-start(f32[64,64,16]{1,2,0:T(8,128)} %gather_fusion.1) | copy-start | bytes 786436
  160.5 5.8 %copy-start.40 = (pred[64]{0:T(512)(128)(4,1)S(1)}, pred[64]{0:T(512)(128)(4,1)}, u32[]{:S(2)}) copy-start(pred[64]{0:T(512)(128)(4,1)} %get-tuple-element.70) | copy-start | bytes 196
  163.8 6.0 %copy-start.7 = (f32[64,64,64]{2,1,0:T(8,128)S(1)}, f32[64,64,64]{2,1,0:T(8,128)}, u32[]{:S(2)}) copy-start(f32[64,64,64]{2,1,0:T(8,128)} %reshape_squeeze.49) | copy-start | bytes 3145732
  163.8 6.0 %copy-start.22 = (f32[64,64,16]{1,2,0:T(8,128)S(1)}, f32[64,64,16]{1,2,0:T(8,128)}, u32[]{:S(2)}) copy-start(f32[64,64,16]{1,2,0:T(8,128)} %gather_fusion.2) | copy-start | bytes 786436
  163.8 6.0 %copy-start.47 = (pred[64]{0:T(512)(128)(4,1)S(1)}, pred[64]{0:T(512)(128)(4,1)}, u32[]{:S(2)}) copy-start(pred[64]{0:T(512)(128)(4,1)} %get-tuple-element.68) | copy-start | bytes 196
  169.7 3.5 copy-start.6
  169.7 3.5 copy-start.21
  169.7 3.5 copy-start.46
  249.1 1.9 copy-start.49
  249.1 2.2 copy-start.27
  249.1 2.5 copy-start.50
  251.0 257.7 %copy-start.2 = (f32[32,64,64]{2,1,0:T(8,128)S(1)}, f32[32,64,64]{2,1,0:T(8,128)}, u32[]{:S(2)}) copy-start(f32[32,64,64]{2,1,0:T(8,128)} %copy-done.1) | copy-start | bytes 1572868
  251.0 257.7 %copy-start.25 = (f32[32,16,64]{2,1,0:T(8,128)S(1)}, f32[32,16,64]{2,1,0:T(8,128)}, u32[]{:S(2)}) copy-start(f32[32,16,64]{2,1,0:T(8,128)} %convolution_add_fusion.7) | copy-start | bytes 393220
  502.1 8.3 %copy-start = (f32[64,64,64]{2,1,0:T(8,128)S(1)}, f32[64,64,64]{2,1,0:T(8,128)}, u32[]{:S(2)}) copy-start(f32[64,64,64]{2,1,0:T(8,128)} %reshape.99) | copy-start | bytes 3145732
  502.1 8.3 %copy-start.17 = (f32[64,16,64]{2,1,0:T(8,128)S(1)}, f32[64,16,64]{2,1,0:T(8,128)}, u32[]{:S(2)}) copy-start(f32[64,16,64]{2,1,0:T(8,128)} %convolution_add_fusion.4) | copy-start | bytes 786436
  513.8 3.4 copy-start.5
  513.8 3.4 copy-start.20
  513.9 3.4 copy-start.45
  517.2 3.7 copy-start.4
  517.2 3.7 copy-start.19
  517.2 3.7 copy-start.44
  520.9 3.5 copy-start.3
  520.9 3.5 copy-start.18
  520.9 3.5 copy-start.43
Sparse Core Ops, SparseCore 0:
  133.4 115.6 all-gather.1
  254.6 247.5 all-reduce.1
where the time goes:
time: 561 us; the launch traced here: 550 us
  waiting for transfers between devices  318 us (57%)
  local copies, waits for them, and re-layouts  106 us (19%)
  matrix products  67.2 us (12%)
  starting transfers between devices  30.1 us (5%)
  between operations  14.4 us (3%)
  other arithmetic  14.2 us (3%)
    psum x1, waiting for transfers between devices, body(): falling_all = lax.psum(spread, 'leaf')  247 us
    all_gather x1, waiting for transfers between devices, body(): everyone = lax.all_gather(offered[:, :, None], 'leaf', axis=2, tiled=True)  71.3 us
    dot_general x24, matrix products, product(): return jnp.einsum(form, first, second, precision=exactly)  60.5 us
    another operation x15, local copies, waits for them, and re-layouts, square(): return flat.reshape(flat.shape[:-1] + (rows_count, cols_count))  33.8 us
    gather x2, local copies, waits for them, and re-layouts, body(): ordered = jnp.take(rhs, order[0], axis=1).reshape(columns, leaves, LEAF)  16.3 us
    ppermute x4, starting transfers between devices, with_halo(): before = lax.ppermute(last, axis, up)  13.6 us
    scatter x2, local copies, waits for them, and re-layouts, body(): jnp.zeros((columns, per_device), jnp.float32).at[:, order[0]]  12.7 us
    ppermute x4, starting transfers between devices, with_halo(): after = lax.ppermute(initial, axis, down)  12.4 us
  transfers between devices with their start and end apart: 13, of which 2 were waited for; matrix products, arithmetic and copies ran while one was open for 21% of the time, Pallas kernels for 0%

commit v1 on v0

v1 whole, which is shorter than its diff:
```python
import functools

import jax
import jax.numpy as jnp
from jax import lax
from jax.experimental import pallas as pl
from jax.experimental.pallas import tpu as pltpu
from jax.sharding import PartitionSpec as P

F32, BF16, I32 = jnp.float32, jnp.bfloat16, jnp.int32
MESH = pl.DeviceIdType.MESH
EXACT = lax.Precision.HIGHEST
NEAR_UNROLL = 2
UP_UNROLL = 8


def iota(shape, dim):
    return lax.broadcasted_iota(I32, shape, dim)


def dot(a, b, precision=None):
    return lax.dot_general(
        a, b, (((1,), (0,)), ((), ())), precision=precision, preferred_element_type=F32
    )


def dot_nt(a, b, precision=None):
    return lax.dot_general(
        a, b, (((1,), (1,)), ((), ())), precision=precision, preferred_element_type=F32
    )


def split(x):
    head = x.astype(BF16)
    return head, (x - head.astype(F32)).astype(BF16)


def low_half(rows):
    return iota((rows, 128), 1) < 64


def swap(x):
    return pltpu.roll(x, 64, 1)


def prepare(block):
    a = jnp.concatenate([block[:, 128 * c : 128 * c + 128] for c in range(32)], axis=0)
    rest = a - a.astype(BF16).astype(F32)
    low = low_half(256)
    first = jnp.where(low, a, rest)
    second = swap(jnp.where(low, rest, a))
    top = jnp.where(low, first, second)
    bottom = jnp.where(low, second, first)
    return jnp.concatenate([top, bottom], axis=0).astype(BF16)


def pack(block):
    return jnp.where(low_half(8), block[0:8], block[8:16])


def unpack(packed):
    low, other = low_half(8), swap(packed)
    return jnp.concatenate(
        [jnp.where(low, packed, other), jnp.where(low, other, packed)], axis=0
    )


def pair(tile):
    low, other = low_half(16), swap(tile)
    return jnp.where(low, tile, other), jnp.where(low, other, tile)


def e_rows(block):
    head, rest = split(block)
    return jnp.concatenate([head, rest], axis=1)


def pick_diagonal(wide, nodes):
    lane_node = iota((16, 512), 1) & 7
    result = wide[0:16]
    for n in range(1, nodes):
        result = jnp.where(lane_node == n, wide[16 * n : 16 * n + 16], result)
    return result


def table_of(tiles):
    head, rest = split(jnp.concatenate(tiles, axis=0))
    return jnp.concatenate([head, rest], axis=1)


def lookup(table, tile_index, lane_index):
    width = lane_index.shape[1]
    hot = jnp.where(iota((128, width), 0) == lane_index, 1.0, 0.0).astype(BF16)
    found = dot(table, jnp.concatenate([hot, hot], axis=0))
    tile_index = jnp.broadcast_to(tile_index, (16, width))
    result = found[0:16]
    for s in range(1, 32):
        result = jnp.where(tile_index == s, found[16 * s : 16 * s + 16], result)
    return result


def find_points(order, inverse):
    def step(j, total):
        row = order[:, pl.ds(pl.multiple_of(j * 512, 512), 512)]
        lane = iota((1, 512), 1)
        n, p = lane >> 6, lane & 63
        parity, c = p & 1, p >> 1
        tile = (j * 4 + parity * 2 + (c >> 4)).astype(F32)
        place = ((c & 15) * 8 + n).astype(F32)
        chosen = iota((32, 512), 0) == (row >> 7)
        rows = jnp.concatenate(
            [jnp.where(chosen, tile, 0.0), jnp.where(chosen, place, 0.0)], axis=0
        ).astype(BF16)
        columns = jnp.where(iota((128, 512), 0) == (row & 127), 1.0, 0.0).astype(BF16)
        return total + dot_nt(rows, columns)

    inverse[...] = lax.fori_loop(0, 8, step, jnp.zeros((64, 128), F32), unroll=2).astype(I32)


def times(lhs_terms, w_terms):
    lhs = jnp.concatenate(lhs_terms, axis=1)
    w = jnp.concatenate([w for term in w_terms for w in (term, term)], axis=1)
    return dot_nt(lhs, w)


def kernel(
    devices,
    rhs_h, order_h, lb_h, near_pick, near_h, t1_h, t2_h, tr_h,
    pick_a, fa_h, pick_b, fb_h, pick_c, fc_h, tt_h, top_source, top_target, tb_h,
    vals, inverse,
    rhs_v, order_v, lb_v, near_v, t1_v, t2_v, tr_v, fa_v, fb_v, fc_v, tt_v, tb4_v,
    tb_v, w_lb, w_t1, w_t2, w_tr, to_d, to_n, diagonal, dmat, table, tiles,
    e_ord, e0, e1, e2, e_down, near_f, far_a, far_b, far_c,
    t_rows, halo_up, halo_down, from_below, from_above,
    a_send, a_buf, b_send, b_buf, c_send, c_buf, d_send, d_buf,
    load_sem, halo_sems, a_ssem, a_rsem, b_ssem, b_rsem, c_ssem, c_rsem, d_ssem, d_rsem,
):
    me = lax.axis_index("leaf")
    count = devices // 8
    inside, group = me & 7, me >> 3
    base = me - inside
    above, below = (me + 1) & (devices - 1), (me + devices - 1) & (devices - 1)
    deep = min(8, count)
    wide = count // deep
    line, depth = group // deep, group & (deep - 1)

    def hops(offset):
        dx, dz = offset
        return min(dx, wide - dx) + min(dz, deep - dz)

    offsets = sorted(((dx, dz) for dx in range(wide) for dz in range(deep)), key=hops)[::-1]
    offsets = [(0, 0)] + offsets[:-1]

    def group_at(q, sign=1):
        dx, dz = offsets[q]
        dx, dz = (dx, dz) if sign > 0 else (wide - dx, deep - dz)
        return ((line + dx) & (wide - 1)) * deep + ((depth + dz) & (deep - 1))

    def mate(q):
        return base + ((inside + q) & 7)

    def far_mate(q):
        return group_at(q) * 8 + inside

    loads = {}
    for number, (name, src, dst) in enumerate(
        (
            ("order", order_h, order_v),
            ("rhs", rhs_h, rhs_v),
            ("lb", lb_h, lb_v),
            ("t1", t1_h, t1_v),
            ("t2", t2_h, t2_v),
            ("tr", tr_h, tr_v),
            ("tt", tt_h, tt_v),
            ("near", near_h, near_v),
            ("tb", tb_h, tb4_v),
            ("fa", fa_h, fa_v),
            ("fb", fb_h, fb_v),
            ("fc", fc_h, fc_v),
        )
    ):
        loads[name] = pltpu.make_async_copy(src, dst, load_sem.at[number])
        loads[name].start()

    barrier = pltpu.get_barrier_semaphore()

    def greet(device):
        pl.semaphore_signal(barrier, inc=1, device_id=(device,), device_id_type=MESH)

    greet(above)
    greet(below)

    @pl.loop(1, 8)
    def _(q):
        greet(mate(q))

    for q in range(1, count):
        greet(far_mate(q))

    n_lane, d_lane = iota((512, 512), 0), iota((512, 512), 1)
    wanted = (d_lane & 7) * 64 + ((d_lane >> 3) & 31) * 2 + (d_lane >> 8)
    to_d[...] = jnp.where(n_lane == wanted, 1.0, 0.0).astype(BF16)
    wanted = (n_lane & 7) * 64 + ((n_lane >> 3) & 31) * 2 + (n_lane >> 8)
    to_n[...] = jnp.where(d_lane == wanted, 1.0, 0.0).astype(BF16)
    diagonal[...] = jnp.where(
        (iota((128, 512), 1) & 7) == (iota((128, 512), 0) >> 4), 1.0, 0.0
    ).astype(BF16)

    loads["rhs"].wait()
    table[...] = table_of([rhs_v[:, 128 * t : 128 * t + 128] for t in range(32)])
    for name in ("order", "lb", "t1", "t2", "tr", "tt"):
        loads[name].wait()

    def group_of(ref, g):
        return ref[pl.ds(pl.multiple_of(g * 8, 8), 8), :]

    for j in range(8):
        row = order_v[:, 512 * j : 512 * j + 512]
        found = lookup(table[...], row >> 7, row & 127)
        for i in range(4):
            tile = found[:, 128 * i : 128 * i + 128]
            tiles[4 * j + i] = tile
            for k, block in enumerate(pair(tile)):
                e_ord[8 * j + 2 * i + k + 1] = e_rows(block)
        w_lb[j] = prepare(group_of(lb_v, j))
        w_t1[j] = prepare(group_of(t1_v, j))
        if j < 4:
            w_t2[j] = prepare(group_of(t2_v, j))
        if j < 2:
            w_tr[j] = prepare(group_of(tr_v, j))

    for j in range(3):
        for c in range(32):
            t_rows[j, c : c + 1, :] = tt_v[j, :, 128 * c : 128 * c + 128]
    sort = jnp.where(
        iota((64, 64), 0) == (iota((64, 64), 1) & 31) * 2 + (iota((64, 64), 1) >> 5), 1.0, 0.0
    ).astype(F32)

    def top_matrix(j):
        rows = t_rows[j]
        return dot(sort, jnp.concatenate([rows[:, :64], rows[:, 64:]], axis=0), EXACT)

    lift = dot(top_matrix(0), dot(top_matrix(1), top_matrix(2), EXACT), EXACT)
    lift_wide = jnp.concatenate([lift, lift], axis=1)
    lift_tall = jnp.concatenate([lift, lift], axis=0)

    def spread_rows(groups):
        x = jnp.concatenate(
            [
                jnp.concatenate([tiles[4 * g + i] for i in range(4)], axis=1)
                for g in range(groups)
            ],
            axis=0,
        )
        head, rest = split(x)
        rows = groups * 16
        moved = dot(jnp.concatenate([head, rest], axis=0), to_d[...]).astype(BF16)
        dmat[0, 0:rows, :] = moved[0:rows]
        dmat[1, 0:rows, :] = moved[rows:]

    def up_group(g, w):
        at = pl.ds(pl.multiple_of(g * 16, 16), 16)
        mask = diagonal[...]
        lhs = jnp.concatenate(
            [
                jnp.concatenate([dmat[0, at, :]] * 8, axis=0) * mask,
                jnp.concatenate([dmat[1, at, :]] * 8, axis=0) * mask,
            ],
            axis=0,
        )
        product = dot(lhs, w)
        both = product[0:128] + product[128:256]
        return both + swap(both)

    def each(groups, unroll, step):
        def body(g, carry):
            step(g)
            return carry

        lax.fori_loop(0, groups, body, 0, unroll=min(unroll, groups))

    halo_down[0] = pack(pair(tiles[0])[0])
    halo_up[0] = pack(pair(tiles[31])[1])

    spread_rows(8)

    def leaf_up(g):
        r = up_group(g, w_lb[g])
        e0[pl.ds(8 * g + 3, 8)] = e_rows(r).reshape(8, 16, 256)
        for i in range(4):
            tiles[4 * g + i] = jnp.where(
                low_half(16), r[32 * i : 32 * i + 16], r[32 * i + 16 : 32 * i + 32]
            )

    each(8, UP_UNROLL, leaf_up)

    def keep_ends(slot, nodes):
        for i in range(3):
            first, last = tiles[i // 2], tiles[(nodes - 3 + i) // 2]
            halo_down[slot + i] = pack(pair(first)[i % 2])
            halo_up[slot + i] = pack(pair(last)[(nodes - 3 + i) % 2])

    keep_ends(1, 64)

    def climb(groups, w_ref, e_ref):
        spread_rows(groups)

        def step(g):
            r = up_group(g, w_ref[g])
            parents = [r[32 * i : 32 * i + 16] + r[32 * i + 16 : 32 * i + 32] for i in range(4)]
            for i in range(2):
                tiles[2 * g + i] = jnp.where(low_half(16), parents[2 * i], parents[2 * i + 1])
            for i in range(4):
                e_ref[4 * g + 3 + i] = e_rows(parents[i])

        each(groups, UP_UNROLL, step)

    climb(8, w_t1, e1)
    keep_ends(4, 32)
    climb(4, w_t2, e2)
    keep_ends(7, 16)

    spread_rows(2)
    rooted = jnp.zeros((16, 128), F32)
    for g in range(2):
        r = up_group(g, w_tr[g])
        for n in range(8):
            rooted = rooted + r[16 * n : 16 * n + 16]
    offered = pack(dot(rooted[:, :64], lift_wide, EXACT))
    a_send[...] = offered
    a_buf[0] = offered

    pl.semaphore_wait(barrier, 2 + 7 + count - 1)

    def remote(src, dst, send, receive, device):
        return pltpu.make_async_remote_copy(
            src_ref=src, dst_ref=dst, send_sem=send, recv_sem=receive,
            device_id=(device,), device_id_type=MESH,
        )

    def a_copy(q):
        return remote(a_send, a_buf.at[q], a_ssem.at[q], a_rsem.at[q], mate(q))

    def b_copy(q):
        return remote(b_send, b_buf.at[group], b_ssem.at[q], b_rsem.at[group], far_mate(q))

    def b_arrival(q):
        origin = group_at(q, -1)
        return remote(b_send, b_buf.at[origin], b_ssem.at[q], b_rsem.at[origin], far_mate(q))

    def c_copy(q):
        return remote(c_send.at[q], c_buf.at[q], c_ssem.at[q], c_rsem.at[q], far_mate(q))

    def d_copy(q):
        return remote(d_send, d_buf.at[q], d_ssem.at[q], d_rsem.at[q], mate(q))

    def over(first, last, action):
        for q in range(first, last):
            action(q)

    over(1, 8, lambda q: a_copy(q).start())
    up_copy = remote(halo_up, from_below, halo_sems.at[0], halo_sems.at[1], above)
    down_copy = remote(halo_down, from_above, halo_sems.at[2], halo_sems.at[3], below)
    up_copy.start()
    down_copy.start()

    find_points(order_v, inverse)
    up_copy.wait_recv()
    down_copy.wait_recv()

    def fill(e_ref, nodes, width, slot):
        for i in range(width):
            lower = jnp.where(me == 0, 0.0, unpack(from_below[slot + i]))
            upper = jnp.where(me == devices - 1, 0.0, unpack(from_above[slot + i]))
            e_ref[i] = e_rows(lower)
            e_ref[nodes + width + i] = e_rows(upper)

    fill(e_ord, 64, 1, 0)
    fill(e0, 64, 3, 1)
    fill(e1, 32, 3, 4)
    fill(e2, 16, 3, 7)

    def partners(g, picks, blocks, e_ref, shift, result):
        lhs, w = [], []
        for s in range(3):
            rows = []
            for n in range(8):
                node = 8 * g + n
                rows.append(e_ref[node + shift(picks[s, node])])
            lhs.append(jnp.concatenate(rows, axis=0))
            w.append(prepare(group_of(blocks.at[s], g)))
        result[g] = pick_diagonal(times(lhs, w), 8)

    def near_shift(pick):
        return pick + 1

    def far_shift(pick):
        return pick + (pick >> 1) * 3

    def near_part(first):
        each(
            4,
            NEAR_UNROLL,
            lambda g: partners(g + first, near_pick, near_v, e_ord, near_shift, near_f),
        )

    loads["near"].wait()
    near_part(0)

    over(1, 8, lambda q: a_copy(q).wait_recv())

    def total_of(buffer, slots):
        result = buffer[0]
        for q in range(1, slots):
            result = result + buffer[q]
        return result

    summed = total_of(a_buf, 8)
    b_send[...] = summed
    b_buf[group] = summed
    over(1, count, lambda q: b_copy(q).start())

    near_part(4)
    loads["tb"].wait()
    tb_v[0:4, :] = tb4_v[...]
    tb_v[4:8, :] = jnp.zeros((4, 4096), F32)
    w_top = prepare(tb_v[...])

    over(1, count, lambda q: b_arrival(q).wait_recv())

    picked = []
    for b in range(4):
        picked.append(e_rows(unpack(b_buf[top_source[b]])))
    coupled = pick_diagonal(times([jnp.concatenate(picked, axis=0)], [w_top]), 4)
    head, rest = split(coupled)
    moved = dot(jnp.concatenate([head, rest], axis=0), to_n[:, 0:256])
    moved = moved[0:16] + moved[16:32]
    packed = []
    for i in range(2):
        packed += [pack(block) for block in pair(moved[:, 128 * i : 128 * i + 128])]
    for q in range(count):
        target = group_at(q)
        part = jnp.zeros((8, 128), F32)
        for b in range(4):
            part = part + jnp.where(jnp.full((8, 128), top_target[b]) == target, packed[b], 0.0)
        if q == 0:
            c_buf[0] = part
        else:
            c_send[q] = part
    over(1, count, lambda q: c_copy(q).start())

    loads["fa"].wait()
    each(8, NEAR_UNROLL, lambda g: partners(g, pick_a, fa_v, e0, far_shift, far_a))

    over(1, count, lambda q: c_copy(q).wait_recv())
    summed = total_of(c_buf, count)
    d_send[...] = summed
    d_buf[0] = summed
    over(1, 8, lambda q: d_copy(q).start())

    loads["fb"].wait()
    each(4, NEAR_UNROLL, lambda g: partners(g, pick_b, fb_v, e1, far_shift, far_b))
    loads["fc"].wait()
    each(2, NEAR_UNROLL, lambda g: partners(g, pick_c, fc_v, e2, far_shift, far_c))

    over(1, 8, lambda q: d_copy(q).wait_recv())
    falling = unpack(total_of(d_buf, 8))
    root_down = dot_nt(falling[:, :64], lift_tall, EXACT)

    def to_e(values, groups):
        head, rest = split(values)
        rows = groups * 16
        moved = dot(jnp.concatenate([head, rest], axis=0), to_n[...])
        for g in range(groups):
            for i in range(4):
                at = slice(128 * i, 128 * i + 128)
                heads = pair(moved[16 * g : 16 * g + 16, at])
                rests = pair(moved[rows + 16 * g : rows + 16 * g + 16, at])
                for k in range(2):
                    node = 8 * g + 2 * i + k
                    e_down[node] = jnp.concatenate(
                        [heads[k].astype(BF16), rests[k].astype(BF16)], axis=1
                    )

    def parents_of(g):
        rows = []
        for n in range(4):
            block = e_down[4 * g + n]
            rows += [block, block]
        return jnp.concatenate(rows, axis=0)

    root_e = e_rows(root_down)
    values = [far_c[g] + times([root_e], [w_tr[g]]) for g in range(2)]
    to_e(jnp.concatenate(values, axis=0), 2)

    def descend(groups, w_ref, far):
        def step(g):
            far[g] = far[g] + pick_diagonal(times([parents_of(g)], [w_ref[g]]), 8)

        each(groups, UP_UNROLL, step)
        to_e(jnp.concatenate([far[g] for g in range(groups)], axis=0), groups)

    descend(4, w_t2, far_b)
    descend(8, w_t1, far_a)

    def leaf_down(g):
        lhs = e_down[pl.ds(8 * g, 8)].reshape(128, 256)
        value = near_f[g] + pick_diagonal(times([lhs], [w_lb[g]]), 8)
        for i in range(4):
            vals[4 * g + i] = value[:, 128 * i : 128 * i + 128]

    each(8, UP_UNROLL, leaf_down)

    up_copy.wait_send()
    down_copy.wait_send()
    over(1, 8, lambda q: a_copy(q).wait_send())
    over(1, count, lambda q: b_copy(q).wait_send())
    over(1, count, lambda q: c_copy(q).wait_send())
    over(1, 8, lambda q: d_copy(q).wait_send())


def restore(vals, inverse, out):
    table = table_of([vals[t] for t in range(32)])
    for j in range(8):
        rows = [inverse[4 * j + i : 4 * j + i + 1, :] for i in range(4)]
        lanes = [inverse[4 * j + i + 32 : 4 * j + i + 33, :] for i in range(4)]
        out[:, 512 * j : 512 * j + 512] = lookup(
            table, jnp.concatenate(rows, axis=1), jnp.concatenate(lanes, axis=1)
        )


def body(devices, *args):
    smem, hbm = pl.BlockSpec(memory_space=pltpu.SMEM), pl.BlockSpec(memory_space=pl.ANY)
    vm, whole = pltpu.VMEM, pl.BlockSpec(memory_space=pltpu.VMEM)
    small = (3, 8, 10, 12, 15, 16)
    count = devices // 8
    big = [0, 1, 2, 4, 5, 6, 7, 9, 11, 13, 14, 17]
    dma = pltpu.SemaphoreType.DMA
    scratch = [vm(args[i].shape, args[i].dtype) for i in big]
    scratch += [
        vm((8, 4096), F32),
        vm((8, 512, 128), BF16),
        vm((8, 512, 128), BF16),
        vm((4, 512, 128), BF16),
        vm((2, 512, 128), BF16),
        vm((512, 512), BF16),
        vm((512, 512), BF16),
        vm((128, 512), BF16),
        vm((2, 128, 512), BF16),
        vm((512, 256), BF16),
        vm((32, 16, 128), F32),
        vm((66, 16, 256), BF16),
        vm((70, 16, 256), BF16),
        vm((38, 16, 256), BF16),
        vm((22, 16, 256), BF16),
        vm((64, 16, 256), BF16),
        vm((8, 16, 512), F32),
        vm((8, 16, 512), F32),
        vm((4, 16, 512), F32),
        vm((2, 16, 512), F32),
        vm((3, 32, 128), F32),
        vm((10, 8, 128), F32),
        vm((10, 8, 128), F32),
        vm((10, 8, 128), F32),
        vm((10, 8, 128), F32),
        vm((8, 128), F32),
        vm((8, 8, 128), F32),
        vm((8, 128), F32),
        vm((count, 8, 128), F32),
        vm((count, 8, 128), F32),
        vm((count, 8, 128), F32),
        vm((8, 128), F32),
        vm((8, 8, 128), F32),
        dma((12,)),
        dma((4,)),
        dma((8,)),
        dma((8,)),
        dma((count,)),
        dma((count,)),
        dma((count,)),
        dma((count,)),
        dma((8,)),
        dma((8,)),
    ]
    vals, inverse = pl.pallas_call(
        functools.partial(kernel, devices),
        out_shape=(
            jax.ShapeDtypeStruct((32, 16, 128), F32),
            jax.ShapeDtypeStruct((64, 128), I32),
        ),
        in_specs=[smem if i in small else hbm for i in range(18)],
        out_specs=(whole, whole),
        scratch_shapes=scratch,
        compiler_params=pltpu.CompilerParams(
            collective_id=0, has_side_effects=True, vmem_limit_bytes=60 * 1024 * 1024
        ),
    )(*args)
    return pl.pallas_call(
        restore,
        out_shape=jax.ShapeDtypeStruct((16, 4096), F32),
        in_specs=[whole] * 2,
        out_specs=whole,
        compiler_params=pltpu.CompilerParams(vmem_limit_bytes=60 * 1024 * 1024),
    )(vals, inverse)


def solution(mesh):
    split_rows, split_columns = P("leaf", None), P(None, "leaf")
    split_middle = P(None, "leaf", None)
    in_specs = (
        split_columns,
        split_rows,
        split_rows,
        split_columns,
        split_middle,
        split_rows,
        split_rows,
        split_rows,
        split_columns,
        split_middle,
        split_columns,
        split_middle,
        split_columns,
        split_middle,
        split_middle,
        P("leaf"),
        P("leaf"),
        split_rows,
    )
    return jax.shard_map(
        functools.partial(body, mesh.shape["leaf"]),
        mesh=mesh,
        in_specs=in_specs,
        out_specs=split_columns,
        check_vma=False,
    )
```

time: 561 us -> 44.3 us (0.08); the launches traced: 550 us -> 44 us
  waiting for transfers between devices: 318 us -> 0 us
  local copies, waits for them, and re-layouts: 106 us -> 0 us
  matrix products: 67.2 us -> 0 us
  Pallas kernels: 0 us -> 44 us
  starting transfers between devices: 30.1 us -> 0 us
  between operations: 14.4 us -> 0.01 us
  other arithmetic: 14.2 us -> 0 us
    psum x1 -> x0, waiting for transfers between devices: 247 us -> none  [body(): falling_all = lax.psum(spread, 'leaf')]
    all_gather x1 -> x0, waiting for transfers between devices: 71.3 us -> none  [body(): everyone = lax.all_gather(offered[:, :, None], 'leaf', axis=2, tiled=True)]
    dot_general x30 -> x0, matrix products: 67.2 us -> none  [the longest x24 60.5 us: product(): return jnp.einsum(form, first, second, precision=exactly)]
    pallas_call x0 -> x2, Pallas kernels: none -> 44 us  [the longest x1 40.9 us: body(): pl.pallas_call(functools.partial(kernel, devices), out_shape=(jax.ShapeDt...]
    another operation x15 -> x0, local copies, waits for them, and re-layouts: 33.8 us -> none  [square(): return flat.reshape(flat.shape[:-1] + (rows_count, cols_count))]
    gather x14 -> x0, local copies, waits for them, and re-layouts: 31.7 us -> none  [the longest x2 16.3 us: body(): ordered = jnp.take(rhs, order[0], axis=1).reshape(columns, leaves, LEAF)]
    ppermute x11 -> x0, starting transfers between devices: 30.1 us -> none  [the longest x4 13.6 us: with_halo(): before = lax.ppermute(last, axis, up)]
    scatter x2 -> x0, local copies, waits for them, and re-layouts: 12.7 us -> none  [body(): jnp.zeros((columns, per_device), jnp.float32).at[:, order[0]]]
  transfers between devices with their start and end apart: 13 -> 0, of which waited for: 2 -> 0; matrix products, arithmetic and copies ran while one was open for 21% -> 0% of each run, Pallas kernels for 0% -> 0%
where the time goes in v1:
time: 44.3 us; the launch traced here: 44 us
  Pallas kernels  44 us (99%)
    pallas_call x1, Pallas kernels, body(): pl.pallas_call(functools.partial(kernel, devices), out_shape=(jax.ShapeDt...  40.9 us
    pallas_call x1, Pallas kernels, body(): pl.pallas_call(restore, out_shape=jax.ShapeDtypeStruct((16, 4096), F32),...  3.07 us

profile of v1, /device:TPU:1, one launch (start us, length us, event | category | flops | bytes accessed | tf_op | source)
XLA Modules:
  0.0 44.0 jit_solution(12558948344290292076)
XLA Ops:
  0.0 40.9 %shard_map.172 = (f32[32,16,128]{2,1,0:T(8,128)}, s32[64,128]{1,0:T(8,128)}) custom-call(f32[16,4096]{1,0:T(8,128)} %rhs_h.1, s32[1,4096]{1,0:T(1,128)} %order_h.1, f32[64,4096]{1,0:T(8,128)} %lb_h.1, s32[3,64]{1,0:T(4,128)} %near_pick.1, f32[3,64,4096]{2,1,0:T(8,128)} %near_h.1, f32[64,4096]{1,0:T(8,128)} %t1_h.1, f32[32,4096]{1,0:T(8,128)} %t2_h.1, ...), custom_call_target="tpu_custom_call" | custom-call | tf_op jit(solution)/shard_map/pallas_call | solution.py:585
  41.0 3.1 %shard_map.173 = f32[16,4096]{1,0:T(8,128)} custom-call(f32[32,16,128]{2,1,0:T(8,128)} %get-tuple-element.7.vals, s32[64,128]{1,0:T(8,128)} %get-tuple-element.8.inverse), custom_call_target="tpu_custom_call" | custom-call | tf_op jit(solution)/shard_map/pallas_call | solution.py:598

commit v2 on v1

--- a/solution.py
+++ b/solution.py
@@ -12,6 +12,8 @@
 EXACT = lax.Precision.HIGHEST
 NEAR_UNROLL = 2
 UP_UNROLL = 8
+DOWN_UNROLL = 4
+Z_UNROLL = 1
 
 
 def iota(shape, dim):
@@ -66,7 +68,7 @@
 
 
 def pair(tile):
-    low, other = low_half(16), swap(tile)
+    low, other = low_half(tile.shape[0]), swap(tile)
     return jnp.where(low, tile, other), jnp.where(low, other, tile)
 
 
@@ -75,11 +77,11 @@
     return jnp.concatenate([head, rest], axis=1)
 
 
-def pick_diagonal(wide, nodes):
-    lane_node = iota((16, 512), 1) & 7
-    result = wide[0:16]
+def pick_diagonal(wide, nodes, rows=16):
+    lane_node = iota((rows, 512), 1) & 7
+    result = wide[0:rows]
     for n in range(1, nodes):
-        result = jnp.where(lane_node == n, wide[16 * n : 16 * n + 16], result)
+        result = jnp.where(lane_node == n, wide[rows * n : rows * n + rows], result)
     return result
 
 
@@ -130,7 +132,7 @@
     vals, inverse,
     rhs_v, order_v, lb_v, near_v, t1_v, t2_v, tr_v, fa_v, fb_v, fc_v, tt_v, tb4_v,
     tb_v, w_lb, w_t1, w_t2, w_tr, to_d, to_n, diagonal, dmat, table, tiles,
-    e_ord, e0, e1, e2, e_down, near_f, far_a, far_b, far_c,
+    e_ord, e0, e1, e2, e_down, z_d, z_e, z_w, lift_rows, near_f, far_a, far_b, far_c,
     t_rows, halo_up, halo_down, from_below, from_above,
     a_send, a_buf, b_send, b_buf, c_send, c_buf, d_send, d_buf,
     load_sem, halo_sems, a_ssem, a_rsem, b_ssem, b_rsem, c_ssem, c_rsem, d_ssem, d_rsem,
@@ -163,24 +165,14 @@
         return group_at(q) * 8 + inside
 
     loads = {}
-    for number, (name, src, dst) in enumerate(
-        (
-            ("order", order_h, order_v),
-            ("rhs", rhs_h, rhs_v),
-            ("lb", lb_h, lb_v),
-            ("t1", t1_h, t1_v),
-            ("t2", t2_h, t2_v),
-            ("tr", tr_h, tr_v),
-            ("tt", tt_h, tt_v),
-            ("near", near_h, near_v),
-            ("tb", tb_h, tb4_v),
-            ("fa", fa_h, fa_v),
-            ("fb", fb_h, fb_v),
-            ("fc", fc_h, fc_v),
-        )
-    ):
-        loads[name] = pltpu.make_async_copy(src, dst, load_sem.at[number])
-        loads[name].start()
+
+    def load(**pairs):
+        for name, (src, dst) in pairs.items():
+            loads[name] = pltpu.make_async_copy(src, dst, load_sem.at[len(loads)])
+            loads[name].start()
+
+    load(order=(order_h, order_v), rhs=(rhs_h, rhs_v), lb=(lb_h, lb_v), t1=(t1_h, t1_v))
+    load(t2=(t2_h, t2_v), tr=(tr_h, tr_v), tt=(tt_h, tt_v))
 
     barrier = pltpu.get_barrier_semaphore()
 
@@ -208,12 +200,18 @@
 
     loads["rhs"].wait()
     table[...] = table_of([rhs_v[:, 128 * t : 128 * t + 128] for t in range(32)])
-    for name in ("order", "lb", "t1", "t2", "tr", "tt"):
-        loads[name].wait()
+    loads["order"].wait()
 
     def group_of(ref, g):
         return ref[pl.ds(pl.multiple_of(g * 8, 8), 8), :]
 
+    split_next = [
+        (name, ref, w, g)
+        for name, ref, w, groups in (
+            ("lb", lb_v, w_lb, 8), ("t1", t1_v, w_t1, 8), ("t2", t2_v, w_t2, 4), ("tr", tr_v, w_tr, 2)
+        )
+        for g in range(groups)
+    ]
     for j in range(8):
         row = order_v[:, 512 * j : 512 * j + 512]
         found = lookup(table[...], row >> 7, row & 127)
@@ -222,13 +220,17 @@
             tiles[4 * j + i] = tile
             for k, block in enumerate(pair(tile)):
                 e_ord[8 * j + 2 * i + k + 1] = e_rows(block)
-        w_lb[j] = prepare(group_of(lb_v, j))
-        w_t1[j] = prepare(group_of(t1_v, j))
-        if j < 4:
-            w_t2[j] = prepare(group_of(t2_v, j))
-        if j < 2:
-            w_tr[j] = prepare(group_of(tr_v, j))
-
+        for _ in range(min(j + 1, 3)):
+            name, ref, w, g = split_next.pop(0)
+            if g == 0:
+                loads[name].wait()
+            w[g] = prepare(group_of(ref, g))
+    while split_next:
+        name, ref, w, g = split_next.pop(0)
+        w[g] = prepare(group_of(ref, g))
+    load(near=(near_h, near_v), fa=(fa_h, fa_v), fb=(fb_h, fb_v), fc=(fc_h, fc_v), tb=(tb_h, tb4_v))
+
+    loads["tt"].wait()
     for j in range(3):
         for c in range(32):
             t_rows[j, c : c + 1, :] = tt_v[j, :, 128 * c : 128 * c + 128]
@@ -242,7 +244,7 @@
 
     lift = dot(top_matrix(0), dot(top_matrix(1), top_matrix(2), EXACT), EXACT)
     lift_wide = jnp.concatenate([lift, lift], axis=1)
-    lift_tall = jnp.concatenate([lift, lift], axis=0)
+    lift_rows[...] = lift
 
     def spread_rows(groups):
         x = jnp.concatenate(
@@ -404,8 +406,66 @@
             lambda g: partners(g + first, near_pick, near_v, e_ord, near_shift, near_f),
         )
 
-    loads["near"].wait()
-    near_part(0)
+    def parents_of(e_ref, g):
+        rows = []
+        for n in range(4):
+            block = e_ref[4 * g + n]
+            rows += [block, block]
+        return jnp.concatenate(rows, axis=0)
+
+    def to_e(source, e_ref, groups, rows, unroll):
+        def step(g):
+            head, rest = split(source[g])
+            moved = dot(jnp.concatenate([head, rest], axis=0), to_n[...])
+            for i in range(4):
+                at = slice(128 * i, 128 * i + 128)
+                heads, rests = pair(moved[0:rows, at]), pair(moved[rows:, at])
+                for k in range(2):
+                    e_ref[8 * g + 2 * i + k] = jnp.concatenate(
+                        [heads[k].astype(BF16), rests[k].astype(BF16)], axis=1
+                    )
+
+        each(groups, unroll, step)
+
+    def compose_two():
+        lift_t = dot_nt(
+            jnp.where(iota((64, 64), 0) == iota((64, 64), 1), 1.0, 0.0).astype(F32),
+            lift_rows[...],
+            EXACT,
+        )
+        start = e_rows(jnp.concatenate([lift_t, lift_t], axis=1))
+        for g in range(2):
+            z_d[g] = times([start], [w_tr[g]])
+        to_e(z_d, z_e, 2, 64, 2)
+
+    def compose(groups, w_ref):
+        def step(g):
+            z_d[g] = pick_diagonal(times([parents_of(z_e, g)], [w_ref[g]]), 8, 64)
+
+        each(groups, Z_UNROLL, step)
+        to_e(z_d, z_e, groups, 64, Z_UNROLL)
+
+    def compose_leaves():
+        def step(g):
+            lhs = z_e[pl.ds(8 * g, 8)].reshape(512, 256)
+            head, rest = split(pick_diagonal(times([lhs], [w_lb[g]]), 8, 64))
+            z_w[g] = jnp.concatenate([head, rest, head, rest], axis=0)
+
+        each(8, Z_UNROLL, step)
+
+    def descend(groups, w_ref, far):
+        def step(g):
+            far[g] = far[g] + pick_diagonal(times([parents_of(e_down, g)], [w_ref[g]]), 8)
+
+        each(groups, DOWN_UNROLL, step)
+        to_e(far, e_down, groups, 16, DOWN_UNROLL)
+
+    compose_two()
+    compose(4, w_t2)
+    loads["fc"].wait()
+    each(2, NEAR_UNROLL, lambda g: partners(g, pick_c, fc_v, e2, far_shift, far_c))
+    loads["fb"].wait()
+    each(4, NEAR_UNROLL, lambda g: partners(g, pick_b, fb_v, e1, far_shift, far_b))
 
     over(1, 8, lambda q: a_copy(q).wait_recv())
 
@@ -420,7 +480,10 @@
     b_buf[group] = summed
     over(1, count, lambda q: b_copy(q).start())
 
-    near_part(4)
+    compose(8, w_t1)
+    compose_leaves()
+    loads["near"].wait()
+    near_part(0)
     loads["tb"].wait()
     tb_v[0:4, :] = tb4_v[...]
     tb_v[4:8, :] = jnp.zeros((4, 4096), F32)
@@ -449,6 +512,7 @@
             c_send[q] = part
     over(1, count, lambda q: c_copy(q).start())
 
+    near_part(4)
     loads["fa"].wait()
     each(8, NEAR_UNROLL, lambda g: partners(g, pick_a, fa_v, e0, far_shift, far_a))
 
@@ -458,58 +522,23 @@
     d_buf[0] = summed
     over(1, 8, lambda q: d_copy(q).start())
 
-    loads["fb"].wait()
-    each(4, NEAR_UNROLL, lambda g: partners(g, pick_b, fb_v, e1, far_shift, far_b))
-    loads["fc"].wait()
-    each(2, NEAR_UNROLL, lambda g: partners(g, pick_c, fc_v, e2, far_shift, far_c))
-
-    over(1, 8, lambda q: d_copy(q).wait_recv())
-    falling = unpack(total_of(d_buf, 8))
-    root_down = dot_nt(falling[:, :64], lift_tall, EXACT)
-
-    def to_e(values, groups):
-        head, rest = split(values)
-        rows = groups * 16
-        moved = dot(jnp.concatenate([head, rest], axis=0), to_n[...])
-        for g in range(groups):
-            for i in range(4):
-                at = slice(128 * i, 128 * i + 128)
-                heads = pair(moved[16 * g : 16 * g + 16, at])
-                rests = pair(moved[rows + 16 * g : rows + 16 * g + 16, at])
-                for k in range(2):
-                    node = 8 * g + 2 * i + k
-                    e_down[node] = jnp.concatenate(
-                        [heads[k].astype(BF16), rests[k].astype(BF16)], axis=1
-                    )
-
-    def parents_of(g):
-        rows = []
-        for n in range(4):
-            block = e_down[4 * g + n]
-            rows += [block, block]
-        return jnp.concatenate(rows, axis=0)
-
-    root_e = e_rows(root_down)
-    values = [far_c[g] + times([root_e], [w_tr[g]]) for g in range(2)]
-    to_e(jnp.concatenate(values, axis=0), 2)
-
-    def descend(groups, w_ref, far):
-        def step(g):
-            far[g] = far[g] + pick_diagonal(times([parents_of(g)], [w_ref[g]]), 8)
-
-        each(groups, UP_UNROLL, step)
-        to_e(jnp.concatenate([far[g] for g in range(groups)], axis=0), groups)
-
+    to_e(far_c, e_down, 2, 16, 2)
     descend(4, w_t2, far_b)
     descend(8, w_t1, far_a)
 
     def leaf_down(g):
         lhs = e_down[pl.ds(8 * g, 8)].reshape(128, 256)
-        value = near_f[g] + pick_diagonal(times([lhs], [w_lb[g]]), 8)
+        near_f[g] = near_f[g] + pick_diagonal(times([lhs], [w_lb[g]]), 8)
+
+    each(8, DOWN_UNROLL, leaf_down)
+
+    over(1, 8, lambda q: d_copy(q).wait_recv())
+    falling = e_rows(unpack(total_of(d_buf, 8)))
+
+    for g in range(8):
+        value = near_f[g] + dot(falling, z_w[g])
         for i in range(4):
             vals[4 * g + i] = value[:, 128 * i : 128 * i + 128]
-
-    each(8, UP_UNROLL, leaf_down)
 
     up_copy.wait_send()
     down_copy.wait_send()
@@ -554,6 +583,10 @@
         vm((38, 16, 256), BF16),
         vm((22, 16, 256), BF16),
         vm((64, 16, 256), BF16),
+        vm((8, 64, 512), F32),
+        vm((64, 64, 256), BF16),
+        vm((8, 256, 512), BF16),
+        vm((64, 64), F32),
         vm((8, 16, 512), F32),
         vm((8, 16, 512), F32),
         vm((4, 16, 512), F32),

time: 44.3 us -> 50.5 us (1.14)
  Pallas kernels: 44 us -> 50.4 us
    pallas_call x1, Pallas kernels: 40.9 us -> 47.3 us  [body(): pl.pallas_call(functools.partial(kernel, devices), out_shape=(jax.ShapeDt...]
where the time goes in v2:
time: 50.5 us; the launch traced here: 50.4 us
  Pallas kernels  50.4 us (100%)
    pallas_call x1, Pallas kernels, body(): pl.pallas_call(functools.partial(kernel, devices), out_shape=(jax.ShapeDt...  47.3 us
    pallas_call x1, Pallas kernels, body(): pl.pallas_call(restore, out_shape=jax.ShapeDtypeStruct((16, 4096), F32),...  3.07 us

profile of v2, /device:TPU:1, one launch (start us, length us, event | category | flops | bytes accessed | tf_op | source)
XLA Modules:
  0.0 50.4 jit_solution(17656099562314502467)
XLA Ops:
  0.0 47.3 %shard_map.172 = (f32[32,16,128]{2,1,0:T(8,128)}, s32[64,128]{1,0:T(8,128)}) custom-call(f32[16,4096]{1,0:T(8,128)} %rhs_h.1, s32[1,4096]{1,0:T(1,128)} %order_h.1, f32[64,4096]{1,0:T(8,128)} %lb_h.1, s32[3,64]{1,0:T(4,128)} %near_pick.1, f32[3,64,4096]{2,1,0:T(8,128)} %near_h.1, f32[64,4096]{1,0:T(8,128)} %t1_h.1, f32[32,4096]{1,0:T(8,128)} %t2_h.1, ...), custom_call_target="tpu_custom_call" | custom-call | tf_op jit(solution)/shard_map/pallas_call | solution.py:618
  47.3 3.1 %shard_map.173 = f32[16,4096]{1,0:T(8,128)} custom-call(f32[32,16,128]{2,1,0:T(8,128)} %get-tuple-element.7.vals, s32[64,128]{1,0:T(8,128)} %get-tuple-element.8.inverse), custom_call_target="tpu_custom_call" | custom-call | tf_op jit(solution)/shard_map/pallas_call | solution.py:631

commit v3 on v1

--- a/solution.py
+++ b/solution.py
@@ -43,10 +43,15 @@
     return pltpu.roll(x, 64, 1)
 
 
-def prepare(block):
-    a = jnp.concatenate([block[:, 128 * c : 128 * c + 128] for c in range(32)], axis=0)
+def prepare(ref, g, half):
+    start = g * 256 + 4 * half
+    return split_rows([ref[pl.ds(start + n, 32, stride=8), :] for n in range(4)])
+
+
+def split_rows(matrices):
+    a = jnp.concatenate(matrices, axis=0)
     rest = a - a.astype(BF16).astype(F32)
-    low = low_half(256)
+    low = low_half(128)
     first = jnp.where(low, a, rest)
     second = swap(jnp.where(low, rest, a))
     top = jnp.where(low, first, second)
@@ -75,10 +80,10 @@
     return jnp.concatenate([head, rest], axis=1)
 
 
-def pick_diagonal(wide, nodes):
-    lane_node = iota((16, 512), 1) & 7
+def pick_diagonal(wide):
+    lane_node = (iota((16, 256), 1) >> 5) & 3
     result = wide[0:16]
-    for n in range(1, nodes):
+    for n in range(1, 4):
         result = jnp.where(lane_node == n, wide[16 * n : 16 * n + 16], result)
     return result
 
@@ -105,8 +110,8 @@
         lane = iota((1, 512), 1)
         n, p = lane >> 6, lane & 63
         parity, c = p & 1, p >> 1
-        tile = (j * 4 + parity * 2 + (c >> 4)).astype(F32)
-        place = ((c & 15) * 8 + n).astype(F32)
+        tile = (j * 4 + (n >> 2) * 2 + parity).astype(F32)
+        place = ((n & 3) * 32 + c).astype(F32)
         chosen = iota((32, 512), 0) == (row >> 7)
         rows = jnp.concatenate(
             [jnp.where(chosen, tile, 0.0), jnp.where(chosen, place, 0.0)], axis=0
@@ -118,9 +123,11 @@
 
 
 def times(lhs_terms, w_terms):
-    lhs = jnp.concatenate(lhs_terms, axis=1)
-    w = jnp.concatenate([w for term in w_terms for w in (term, term)], axis=1)
-    return dot_nt(lhs, w)
+    rows = lhs_terms[0].shape[0]
+    heads = jnp.concatenate([lhs[:, :128] for lhs in lhs_terms], axis=1)
+    rests = jnp.concatenate([lhs[:, 128:] for lhs in lhs_terms], axis=1)
+    both = dot_nt(jnp.concatenate([heads, rests], axis=0), jnp.concatenate(w_terms, axis=1))
+    return both[:rows] + both[rows:]
 
 
 def kernel(
@@ -128,10 +135,10 @@
     rhs_h, order_h, lb_h, near_pick, near_h, t1_h, t2_h, tr_h,
     pick_a, fa_h, pick_b, fb_h, pick_c, fc_h, tt_h, top_source, top_target, tb_h,
     vals, inverse,
-    rhs_v, order_v, lb_v, near_v, t1_v, t2_v, tr_v, fa_v, fb_v, fc_v, tt_v, tb4_v,
-    tb_v, w_lb, w_t1, w_t2, w_tr, to_d, to_n, diagonal, dmat, table, tiles,
+    rhs_v, order_v, lb_v, near_v, t1_v, t2_v, tr_v, fa_v, fb_v, fc_v, tt_v, tb_v,
+    w_lb, w_t1, w_t2, w_tr, to_d, to_n, diagonal, dmat, table, tiles,
     e_ord, e0, e1, e2, e_down, near_f, far_a, far_b, far_c,
-    t_rows, halo_up, halo_down, from_below, from_above,
+    halo_up, halo_down, from_below, from_above,
     a_send, a_buf, b_send, b_buf, c_send, c_buf, d_send, d_buf,
     load_sem, halo_sems, a_ssem, a_rsem, b_ssem, b_rsem, c_ssem, c_rsem, d_ssem, d_rsem,
 ):
@@ -163,24 +170,14 @@
         return group_at(q) * 8 + inside
 
     loads = {}
-    for number, (name, src, dst) in enumerate(
-        (
-            ("order", order_h, order_v),
-            ("rhs", rhs_h, rhs_v),
-            ("lb", lb_h, lb_v),
-            ("t1", t1_h, t1_v),
-            ("t2", t2_h, t2_v),
-            ("tr", tr_h, tr_v),
-            ("tt", tt_h, tt_v),
-            ("near", near_h, near_v),
-            ("tb", tb_h, tb4_v),
-            ("fa", fa_h, fa_v),
-            ("fb", fb_h, fb_v),
-            ("fc", fc_h, fc_v),
-        )
-    ):
-        loads[name] = pltpu.make_async_copy(src, dst, load_sem.at[number])
-        loads[name].start()
+
+    def load(**pairs):
+        for name, (src, dst) in pairs.items():
+            loads[name] = pltpu.make_async_copy(src, dst, load_sem.at[len(loads)])
+            loads[name].start()
+
+    load(order=(order_h, order_v), rhs=(rhs_h, rhs_v), lb=(lb_h, lb_v), t1=(t1_h, t1_v))
+    load(t2=(t2_h, t2_v), tr=(tr_h, tr_v), tt=(tt_h, tt_v))
 
     barrier = pltpu.get_barrier_semaphore()
 
@@ -197,22 +194,34 @@
     for q in range(1, count):
         greet(far_mate(q))
 
-    n_lane, d_lane = iota((512, 512), 0), iota((512, 512), 1)
-    wanted = (d_lane & 7) * 64 + ((d_lane >> 3) & 31) * 2 + (d_lane >> 8)
-    to_d[...] = jnp.where(n_lane == wanted, 1.0, 0.0).astype(BF16)
-    wanted = (n_lane & 7) * 64 + ((n_lane >> 3) & 31) * 2 + (n_lane >> 8)
-    to_n[...] = jnp.where(d_lane == wanted, 1.0, 0.0).astype(BF16)
+    rows, lanes = iota((256, 256), 0), iota((256, 256), 1)
+
+    def natural(place):
+        return ((place >> 5) & 3) * 64 + (place & 31) * 2 + (place >> 7)
+
+    to_d[...] = jnp.where(rows == natural(lanes), 1.0, 0.0).astype(BF16)
+    to_n[...] = jnp.where(lanes == natural(rows), 1.0, 0.0).astype(BF16)
     diagonal[...] = jnp.where(
-        (iota((128, 512), 1) & 7) == (iota((128, 512), 0) >> 4), 1.0, 0.0
+        ((iota((64, 256), 1) >> 5) & 3) == (iota((64, 256), 0) >> 4), 1.0, 0.0
     ).astype(BF16)
 
     loads["rhs"].wait()
     table[...] = table_of([rhs_v[:, 128 * t : 128 * t + 128] for t in range(32)])
-    for name in ("order", "lb", "t1", "t2", "tr", "tt"):
-        loads[name].wait()
-
-    def group_of(ref, g):
-        return ref[pl.ds(pl.multiple_of(g * 8, 8), 8), :]
+    loads["order"].wait()
+    split_next = [
+        (name, ref, w, g)
+        for name, ref, w, groups in (
+            ("lb", lb_v, w_lb, 8), ("t1", t1_v, w_t1, 8), ("t2", t2_v, w_t2, 4), ("tr", tr_v, w_tr, 2)
+        )
+        for g in range(groups)
+    ]
+
+    def split_one():
+        name, ref, w, g = split_next.pop(0)
+        if g == 0:
+            loads[name].wait()
+        for half in range(2):
+            w[g, :, 128 * half : 128 * half + 128] = prepare(ref, g, half)
 
     for j in range(8):
         row = order_v[:, 512 * j : 512 * j + 512]
@@ -222,22 +231,19 @@
             tiles[4 * j + i] = tile
             for k, block in enumerate(pair(tile)):
                 e_ord[8 * j + 2 * i + k + 1] = e_rows(block)
-        w_lb[j] = prepare(group_of(lb_v, j))
-        w_t1[j] = prepare(group_of(t1_v, j))
-        if j < 4:
-            w_t2[j] = prepare(group_of(t2_v, j))
-        if j < 2:
-            w_tr[j] = prepare(group_of(tr_v, j))
-
-    for j in range(3):
-        for c in range(32):
-            t_rows[j, c : c + 1, :] = tt_v[j, :, 128 * c : 128 * c + 128]
+        for _ in range(min(j + 1, 3)):
+            split_one()
+    while split_next:
+        split_one()
+    load(near=(near_h, near_v), fa=(fa_h, fa_v), fb=(fb_h, fb_v), fc=(fc_h, fc_v), tb=(tb_h, tb_v))
+
+    loads["tt"].wait()
     sort = jnp.where(
         iota((64, 64), 0) == (iota((64, 64), 1) & 31) * 2 + (iota((64, 64), 1) >> 5), 1.0, 0.0
     ).astype(F32)
 
     def top_matrix(j):
-        rows = t_rows[j]
+        rows = tt_v[j]
         return dot(sort, jnp.concatenate([rows[:, :64], rows[:, 64:]], axis=0), EXACT)
 
     lift = dot(top_matrix(0), dot(top_matrix(1), top_matrix(2), EXACT), EXACT)
@@ -245,32 +251,31 @@
     lift_tall = jnp.concatenate([lift, lift], axis=0)
 
     def spread_rows(groups):
+        quads = 2 * groups
         x = jnp.concatenate(
-            [
-                jnp.concatenate([tiles[4 * g + i] for i in range(4)], axis=1)
-                for g in range(groups)
-            ],
-            axis=0,
+            [jnp.concatenate([tiles[2 * q], tiles[2 * q + 1]], axis=1) for q in range(quads)], axis=0
         )
-        head, rest = split(x)
-        rows = groups * 16
-        moved = dot(jnp.concatenate([head, rest], axis=0), to_d[...]).astype(BF16)
-        dmat[0, 0:rows, :] = moved[0:rows]
-        dmat[1, 0:rows, :] = moved[rows:]
+        moved = dot(jnp.concatenate(split(x), axis=0), to_d[...]).astype(BF16)
+        dmat[0, 0:quads] = moved[0 : 16 * quads].reshape(quads, 16, 256)
+        dmat[1, 0:quads] = moved[16 * quads :].reshape(quads, 16, 256)
 
     def up_group(g, w):
-        at = pl.ds(pl.multiple_of(g * 16, 16), 16)
         mask = diagonal[...]
         lhs = jnp.concatenate(
             [
-                jnp.concatenate([dmat[0, at, :]] * 8, axis=0) * mask,
-                jnp.concatenate([dmat[1, at, :]] * 8, axis=0) * mask,
+                jnp.concatenate([dmat[part, 2 * g + half]] * 4, axis=0) * mask
+                for half in range(2)
+                for part in range(2)
             ],
             axis=0,
         )
         product = dot(lhs, w)
-        both = product[0:128] + product[128:256]
-        return both + swap(both)
+        results = []
+        for half in range(2):
+            at = slice(128 * half, 128 * half + 128)
+            both = product[128 * half : 128 * half + 64, at] + product[128 * half + 64 : 128 * half + 128, at]
+            results.append(both + swap(both))
+        return jnp.concatenate(results, axis=0)
 
     def each(groups, unroll, step):
         def body(g, carry):
@@ -381,15 +386,16 @@
     fill(e2, 16, 3, 7)
 
     def partners(g, picks, blocks, e_ref, shift, result):
-        lhs, w = [], []
-        for s in range(3):
-            rows = []
-            for n in range(8):
-                node = 8 * g + n
-                rows.append(e_ref[node + shift(picks[s, node])])
-            lhs.append(jnp.concatenate(rows, axis=0))
-            w.append(prepare(group_of(blocks.at[s], g)))
-        result[g] = pick_diagonal(times(lhs, w), 8)
+        for half in range(2):
+            lhs, w = [], []
+            for s in range(3):
+                rows = []
+                for n in range(4):
+                    node = 8 * g + 4 * half + n
+                    rows.append(e_ref[node + shift(picks[s, node])])
+                lhs.append(jnp.concatenate(rows, axis=0))
+                w.append(prepare(blocks.at[s], g, half))
+            result[2 * g + half] = pick_diagonal(times(lhs, w))
 
     def near_shift(pick):
         return pick + 1
@@ -422,18 +428,15 @@
 
     near_part(4)
     loads["tb"].wait()
-    tb_v[0:4, :] = tb4_v[...]
-    tb_v[4:8, :] = jnp.zeros((4, 4096), F32)
-    w_top = prepare(tb_v[...])
+    w_top = split_rows([tb_v[pl.ds(n, 32, stride=4), :] for n in range(4)])
 
     over(1, count, lambda q: b_arrival(q).wait_recv())
 
     picked = []
     for b in range(4):
         picked.append(e_rows(unpack(b_buf[top_source[b]])))
-    coupled = pick_diagonal(times([jnp.concatenate(picked, axis=0)], [w_top]), 4)
-    head, rest = split(coupled)
-    moved = dot(jnp.concatenate([head, rest], axis=0), to_n[:, 0:256])
+    coupled = pick_diagonal(times([jnp.concatenate(picked, axis=0)], [w_top]))
+    moved = dot(jnp.concatenate(split(coupled), axis=0), to_n[...])
     moved = moved[0:16] + moved[16:32]
     packed = []
     for i in range(2):
@@ -467,47 +470,51 @@
     falling = unpack(total_of(d_buf, 8))
     root_down = dot_nt(falling[:, :64], lift_tall, EXACT)
 
-    def to_e(values, groups):
-        head, rest = split(values)
-        rows = groups * 16
-        moved = dot(jnp.concatenate([head, rest], axis=0), to_n[...])
-        for g in range(groups):
-            for i in range(4):
+    def to_e(values, quads):
+        moved = dot(jnp.concatenate(split(values), axis=0), to_n[...])
+        rows = 16 * quads
+        for q in range(quads):
+            for i in range(2):
                 at = slice(128 * i, 128 * i + 128)
-                heads = pair(moved[16 * g : 16 * g + 16, at])
-                rests = pair(moved[rows + 16 * g : rows + 16 * g + 16, at])
+                heads = pair(moved[16 * q : 16 * q + 16, at])
+                rests = pair(moved[rows + 16 * q : rows + 16 * q + 16, at])
                 for k in range(2):
-                    node = 8 * g + 2 * i + k
-                    e_down[node] = jnp.concatenate(
+                    e_down[4 * q + 2 * i + k] = jnp.concatenate(
                         [heads[k].astype(BF16), rests[k].astype(BF16)], axis=1
                     )
 
-    def parents_of(g):
-        rows = []
-        for n in range(4):
-            block = e_down[4 * g + n]
-            rows += [block, block]
-        return jnp.concatenate(rows, axis=0)
+    def half_of(w_ref, g, half):
+        return w_ref[g, :, 128 * half : 128 * half + 128]
 
     root_e = e_rows(root_down)
-    values = [far_c[g] + times([root_e], [w_tr[g]]) for g in range(2)]
-    to_e(jnp.concatenate(values, axis=0), 2)
+    values = [
+        far_c[2 * g + half] + times([root_e], [half_of(w_tr, g, half)])
+        for g in range(2)
+        for half in range(2)
+    ]
+    to_e(jnp.concatenate(values, axis=0), 4)
 
     def descend(groups, w_ref, far):
         def step(g):
-            far[g] = far[g] + pick_diagonal(times([parents_of(g)], [w_ref[g]]), 8)
+            for half in range(2):
+                q = 2 * g + half
+                first, second = e_down[2 * q], e_down[2 * q + 1]
+                lhs = jnp.concatenate([first, first, second, second], axis=0)
+                far[q] = far[q] + pick_diagonal(times([lhs], [half_of(w_ref, g, half)]))
 
         each(groups, UP_UNROLL, step)
-        to_e(jnp.concatenate([far[g] for g in range(groups)], axis=0), groups)
+        to_e(jnp.concatenate([far[q] for q in range(2 * groups)], axis=0), 2 * groups)
 
     descend(4, w_t2, far_b)
     descend(8, w_t1, far_a)
 
     def leaf_down(g):
-        lhs = e_down[pl.ds(8 * g, 8)].reshape(128, 256)
-        value = near_f[g] + pick_diagonal(times([lhs], [w_lb[g]]), 8)
-        for i in range(4):
-            vals[4 * g + i] = value[:, 128 * i : 128 * i + 128]
+        for half in range(2):
+            q = 2 * g + half
+            lhs = e_down[pl.ds(4 * q, 4)].reshape(64, 256)
+            value = near_f[q] + pick_diagonal(times([lhs], [half_of(w_lb, g, half)]))
+            for i in range(2):
+                vals[2 * q + i] = value[:, 128 * i : 128 * i + 128]
 
     each(8, UP_UNROLL, leaf_down)
 
@@ -529,24 +536,31 @@
         )
 
 
+def lay_out(flat):
+    lead, nodes = flat.shape[:-2], flat.shape[-2]
+    n = min(nodes, 8)
+    rows = jnp.swapaxes(flat.reshape(lead + (nodes // n, n, 32, 128)), -3, -2)
+    return rows.reshape(lead + (nodes * 32, 128))
+
+
 def body(devices, *args):
     smem, hbm = pl.BlockSpec(memory_space=pltpu.SMEM), pl.BlockSpec(memory_space=pl.ANY)
     vm, whole = pltpu.VMEM, pl.BlockSpec(memory_space=pltpu.VMEM)
+    args = [lay_out(a) if i in (2, 4, 5, 6, 7, 9, 11, 13, 14, 17) else a for i, a in enumerate(args)]
     small = (3, 8, 10, 12, 15, 16)
     count = devices // 8
     big = [0, 1, 2, 4, 5, 6, 7, 9, 11, 13, 14, 17]
     dma = pltpu.SemaphoreType.DMA
     scratch = [vm(args[i].shape, args[i].dtype) for i in big]
     scratch += [
-        vm((8, 4096), F32),
-        vm((8, 512, 128), BF16),
-        vm((8, 512, 128), BF16),
-        vm((4, 512, 128), BF16),
-        vm((2, 512, 128), BF16),
-        vm((512, 512), BF16),
-        vm((512, 512), BF16),
-        vm((128, 512), BF16),
-        vm((2, 128, 512), BF16),
+        vm((8, 256, 256), BF16),
+        vm((8, 256, 256), BF16),
+        vm((4, 256, 256), BF16),
+        vm((2, 256, 256), BF16),
+        vm((256, 256), BF16),
+        vm((256, 256), BF16),
+        vm((64, 256), BF16),
+        vm((2, 16, 16, 256), BF16),
         vm((512, 256), BF16),
         vm((32, 16, 128), F32),
         vm((66, 16, 256), BF16),
@@ -554,11 +568,10 @@
         vm((38, 16, 256), BF16),
         vm((22, 16, 256), BF16),
         vm((64, 16, 256), BF16),
-        vm((8, 16, 512), F32),
-        vm((8, 16, 512), F32),
-        vm((4, 16, 512), F32),
-        vm((2, 16, 512), F32),
-        vm((3, 32, 128), F32),
+        vm((16, 16, 256), F32),
+        vm((16, 16, 256), F32),
+        vm((8, 16, 256), F32),
+        vm((4, 16, 256), F32),
         vm((10, 8, 128), F32),
         vm((10, 8, 128), F32),
         vm((10, 8, 128), F32),

time: 44.3 us -> 42.8 us (0.966)
  Pallas kernels: 44 us -> 42.5 us
    pallas_call x1, Pallas kernels: 40.9 us -> 39.5 us  [body(): pl.pallas_call(functools.partial(kernel, devices), out_shape=(jax.ShapeDt...]
where the time goes in v3:
time: 42.8 us; the launch traced here: 42.5 us
  Pallas kernels  42.5 us (99%)
    pallas_call x1, Pallas kernels, body(): pl.pallas_call(functools.partial(kernel, devices), out_shape=(jax.ShapeDt...  39.5 us
    pallas_call x1, Pallas kernels, body(): pl.pallas_call(restore, out_shape=jax.ShapeDtypeStruct((16, 4096), F32),...  3.07 us

profile of v3, /device:TPU:1, one launch (start us, length us, event | category | flops | bytes accessed | tf_op | source)
XLA Modules:
  0.0 42.5 jit_solution(6971648195940819727)
XLA Ops:
  0.0 39.5 %shard_map.172 = (f32[32,16,128]{2,1,0:T(8,128)}, s32[64,128]{1,0:T(8,128)}) custom-call(f32[16,4096]{1,0:T(8,128)} %rhs_h.1, s32[1,4096]{1,0:T(1,128)} %order_h.1, f32[2048,128]{1,0:T(8,128)} %bitcast.49, s32[3,64]{1,0:T(4,128)} %near_pick.1, f32[3,2048,128]{2,1,0:T(8,128)} %bitcast.46, f32[2048,128]{1,0:T(8,128)} %bitcast.50, f32[1024,128]{1,0:T(8,128)} %bitcast.52, ...), custom_call_target="tpu_custom_call" | custom-call | tf_op jit(solution)/shard_map/pallas_call | solution.py:598
  39.5 3.1 %shard_map.173 = f32[16,4096]{1,0:T(8,128)} custom-call(f32[32,16,128]{2,1,0:T(8,128)} %get-tuple-element.7.vals, s32[64,128]{1,0:T(8,128)} %get-tuple-element.8.inverse), custom_call_target="tpu_custom_call" | custom-call | tf_op jit(solution)/shard_map/pallas_call | solution.py:611

commit v4 on v3

--- a/solution.py
+++ b/solution.py
@@ -50,13 +50,12 @@
 
 def split_rows(matrices):
     a = jnp.concatenate(matrices, axis=0)
-    rest = a - a.astype(BF16).astype(F32)
+    head = a.astype(BF16)
+    rest = (a - head.astype(F32)).astype(BF16)
     low = low_half(128)
-    first = jnp.where(low, a, rest)
-    second = swap(jnp.where(low, rest, a))
-    top = jnp.where(low, first, second)
-    bottom = jnp.where(low, second, first)
-    return jnp.concatenate([top, bottom], axis=0).astype(BF16)
+    top = jnp.where(low, head, swap(rest))
+    bottom = jnp.where(low, swap(head), rest)
+    return jnp.concatenate([top, bottom], axis=0)
 
 
 def pack(block):

time: 42.8 us -> 42.3 us (0.988)
    pallas_call x1, Pallas kernels: 39.5 us -> 39 us  [body(): pl.pallas_call(functools.partial(kernel, devices), out_shape=(jax.ShapeDt...]
where the time goes in v4:
time: 42.3 us; the launch traced here: 42.1 us
  Pallas kernels  42.1 us (100%)
    pallas_call x1, Pallas kernels, body(): pl.pallas_call(functools.partial(kernel, devices), out_shape=(jax.ShapeDt...  39 us
    pallas_call x1, Pallas kernels, body(): pl.pallas_call(restore, out_shape=jax.ShapeDtypeStruct((16, 4096), F32),...  3.07 us

profile of v4, /device:TPU:1, one launch (start us, length us, event | category | flops | bytes accessed | tf_op | source)
XLA Modules:
  0.0 42.1 jit_solution(14755280079139156429)
XLA Ops:
  0.0 39.0 %shard_map.172 = (f32[32,16,128]{2,1,0:T(8,128)}, s32[64,128]{1,0:T(8,128)}) custom-call(f32[16,4096]{1,0:T(8,128)} %rhs_h.1, s32[1,4096]{1,0:T(1,128)} %order_h.1, f32[2048,128]{1,0:T(8,128)} %bitcast.49, s32[3,64]{1,0:T(4,128)} %near_pick.1, f32[3,2048,128]{2,1,0:T(8,128)} %bitcast.46, f32[2048,128]{1,0:T(8,128)} %bitcast.50, f32[1024,128]{1,0:T(8,128)} %bitcast.52, ...), custom_call_target="tpu_custom_call" | custom-call | tf_op jit(solution)/shard_map/pallas_call | solution.py:597
  39.0 3.1 %shard_map.173 = f32[16,4096]{1,0:T(8,128)} custom-call(f32[32,16,128]{2,1,0:T(8,128)} %get-tuple-element.7.vals, s32[64,128]{1,0:T(8,128)} %get-tuple-element.8.inverse), custom_call_target="tpu_custom_call" | custom-call | tf_op jit(solution)/shard_map/pallas_call | solution.py:610

commit v5 on v4

--- a/solution.py
+++ b/solution.py
@@ -12,6 +12,8 @@
 EXACT = lax.Precision.HIGHEST
 NEAR_UNROLL = 2
 UP_UNROLL = 8
+DOWN_UNROLL = 4
+Z_UNROLL = 2
 
 
 def iota(shape, dim):
@@ -70,7 +72,7 @@
 
 
 def pair(tile):
-    low, other = low_half(16), swap(tile)
+    low, other = low_half(tile.shape[0]), swap(tile)
     return jnp.where(low, tile, other), jnp.where(low, other, tile)
 
 
@@ -79,11 +81,11 @@
     return jnp.concatenate([head, rest], axis=1)
 
 
-def pick_diagonal(wide):
-    lane_node = (iota((16, 256), 1) >> 5) & 3
-    result = wide[0:16]
+def pick_diagonal(wide, rows=16):
+    lane_node = (iota((rows, 256), 1) >> 5) & 3
+    result = wide[0:rows]
     for n in range(1, 4):
-        result = jnp.where(lane_node == n, wide[16 * n : 16 * n + 16], result)
+        result = jnp.where(lane_node == n, wide[rows * n : rows * n + rows], result)
     return result
 
 
@@ -136,7 +138,7 @@
     vals, inverse,
     rhs_v, order_v, lb_v, near_v, t1_v, t2_v, tr_v, fa_v, fb_v, fc_v, tt_v, tb_v,
     w_lb, w_t1, w_t2, w_tr, to_d, to_n, diagonal, dmat, table, tiles,
-    e_ord, e0, e1, e2, e_down, near_f, far_a, far_b, far_c,
+    e_ord, e0, e1, e2, e_down, z_d, z_e, z_w, near_f, far_a, far_b, far_c,
     halo_up, halo_down, from_below, from_above,
     a_send, a_buf, b_send, b_buf, c_send, c_buf, d_send, d_buf,
     load_sem, halo_sems, a_ssem, a_rsem, b_ssem, b_rsem, c_ssem, c_rsem, d_ssem, d_rsem,
@@ -247,7 +249,6 @@
 
     lift = dot(top_matrix(0), dot(top_matrix(1), top_matrix(2), EXACT), EXACT)
     lift_wide = jnp.concatenate([lift, lift], axis=1)
-    lift_tall = jnp.concatenate([lift, lift], axis=0)
 
     def spread_rows(groups):
         quads = 2 * groups
@@ -409,8 +410,90 @@
             lambda g: partners(g + first, near_pick, near_v, e_ord, near_shift, near_f),
         )
 
-    loads["near"].wait()
-    near_part(0)
+    def half_of(w_ref, g, half):
+        return w_ref[g, :, 128 * half : 128 * half + 128]
+
+    def times_wide(lhs, w):
+        return dot_nt(lhs, jnp.concatenate([w, w], axis=1))
+
+    def z_to_e(groups):
+        def step(g):
+            for half in range(2):
+                q = 2 * g + half
+                moved = dot(jnp.concatenate(split(z_d[q]), axis=0), to_n[...])
+                for i in range(2):
+                    at = slice(128 * i, 128 * i + 128)
+                    heads, rests = pair(moved[0:64, at]), pair(moved[64:, at])
+                    for k in range(2):
+                        z_e[4 * q + 2 * i + k] = jnp.concatenate(
+                            [heads[k].astype(BF16), rests[k].astype(BF16)], axis=1
+                        )
+
+        each(groups, Z_UNROLL, step)
+
+    def compose_two():
+        identity = jnp.where(iota((64, 64), 0) == iota((64, 64), 1), 1.0, 0.0).astype(F32)
+        lift_t = dot_nt(identity, lift, EXACT)
+        start = e_rows(jnp.concatenate([lift_t, lift_t], axis=1))
+        for q in range(4):
+            z_d[q] = times_wide(start, half_of(w_tr, q // 2, q % 2))
+        z_to_e(2)
+
+    def compose(groups, w_ref):
+        def step(g):
+            for half in range(2):
+                q = 2 * g + half
+                first, second = z_e[2 * q], z_e[2 * q + 1]
+                lhs = jnp.concatenate([first, first, second, second], axis=0)
+                z_d[q] = pick_diagonal(times_wide(lhs, half_of(w_ref, g, half)), 64)
+
+        each(groups, Z_UNROLL, step)
+        z_to_e(groups)
+
+    def compose_leaves():
+        def step(g):
+            for half in range(2):
+                q = 2 * g + half
+                lhs = z_e[pl.ds(4 * q, 4)].reshape(256, 256)
+                head, rest = split(
+                    pick_diagonal(times_wide(lhs, half_of(w_lb, g, half)), 64)
+                )
+                z_w[q] = jnp.concatenate([head, rest, head, rest], axis=0)
+
+        each(8, Z_UNROLL, step)
+
+    def to_e(values, quads):
+        moved = dot(jnp.concatenate(split(values), axis=0), to_n[...])
+        rows = 16 * quads
+        for q in range(quads):
+            for i in range(2):
+                at = slice(128 * i, 128 * i + 128)
+                heads = pair(moved[16 * q : 16 * q + 16, at])
+                rests = pair(moved[rows + 16 * q : rows + 16 * q + 16, at])
+                for k in range(2):
+                    e_down[4 * q + 2 * i + k] = jnp.concatenate(
+                        [heads[k].astype(BF16), rests[k].astype(BF16)], axis=1
+                    )
+
+    def descend(groups, w_ref, far):
+        def step(g):
+            for half in range(2):
+                q = 2 * g + half
+                first, second = e_down[2 * q], e_down[2 * q + 1]
+                lhs = jnp.concatenate([first, first, second, second], axis=0)
+                far[q] = far[q] + pick_diagonal(times([lhs], [half_of(w_ref, g, half)]))
+
+        each(groups, DOWN_UNROLL, step)
+        to_e(jnp.concatenate([far[q] for q in range(2 * groups)], axis=0), 2 * groups)
+
+    def leaf_down(g):
+        for half in range(2):
+            q = 2 * g + half
+            lhs = e_down[pl.ds(4 * q, 4)].reshape(64, 256)
+            near_f[q] = near_f[q] + pick_diagonal(times([lhs], [half_of(w_lb, g, half)]))
+
+    compose_two()
+    compose(4, w_t2)
 
     over(1, 8, lambda q: a_copy(q).wait_recv())
 
@@ -425,6 +508,9 @@
     b_buf[group] = summed
     over(1, count, lambda q: b_copy(q).start())
 
+    compose(8, w_t1)
+    loads["near"].wait()
+    near_part(0)
     near_part(4)
     loads["tb"].wait()
     w_top = split_rows([tb_v[pl.ds(n, 32, stride=4), :] for n in range(4)])
@@ -451,6 +537,11 @@
             c_send[q] = part
     over(1, count, lambda q: c_copy(q).start())
 
+    compose_leaves()
+    loads["fc"].wait()
+    each(2, NEAR_UNROLL, lambda g: partners(g, pick_c, fc_v, e2, far_shift, far_c))
+    loads["fb"].wait()
+    each(4, NEAR_UNROLL, lambda g: partners(g, pick_b, fb_v, e1, far_shift, far_b))
     loads["fa"].wait()
     each(8, NEAR_UNROLL, lambda g: partners(g, pick_a, fa_v, e0, far_shift, far_a))
 
@@ -460,62 +551,17 @@
     d_buf[0] = summed
     over(1, 8, lambda q: d_copy(q).start())
 
-    loads["fb"].wait()
-    each(4, NEAR_UNROLL, lambda g: partners(g, pick_b, fb_v, e1, far_shift, far_b))
-    loads["fc"].wait()
-    each(2, NEAR_UNROLL, lambda g: partners(g, pick_c, fc_v, e2, far_shift, far_c))
-
-    over(1, 8, lambda q: d_copy(q).wait_recv())
-    falling = unpack(total_of(d_buf, 8))
-    root_down = dot_nt(falling[:, :64], lift_tall, EXACT)
-
-    def to_e(values, quads):
-        moved = dot(jnp.concatenate(split(values), axis=0), to_n[...])
-        rows = 16 * quads
-        for q in range(quads):
-            for i in range(2):
-                at = slice(128 * i, 128 * i + 128)
-                heads = pair(moved[16 * q : 16 * q + 16, at])
-                rests = pair(moved[rows + 16 * q : rows + 16 * q + 16, at])
-                for k in range(2):
-                    e_down[4 * q + 2 * i + k] = jnp.concatenate(
-                        [heads[k].astype(BF16), rests[k].astype(BF16)], axis=1
-                    )
-
-    def half_of(w_ref, g, half):
-        return w_ref[g, :, 128 * half : 128 * half + 128]
-
-    root_e = e_rows(root_down)
-    values = [
-        far_c[2 * g + half] + times([root_e], [half_of(w_tr, g, half)])
-        for g in range(2)
-        for half in range(2)
-    ]
-    to_e(jnp.concatenate(values, axis=0), 4)
-
-    def descend(groups, w_ref, far):
-        def step(g):
-            for half in range(2):
-                q = 2 * g + half
-                first, second = e_down[2 * q], e_down[2 * q + 1]
-                lhs = jnp.concatenate([first, first, second, second], axis=0)
-                far[q] = far[q] + pick_diagonal(times([lhs], [half_of(w_ref, g, half)]))
-
-        each(groups, UP_UNROLL, step)
-        to_e(jnp.concatenate([far[q] for q in range(2 * groups)], axis=0), 2 * groups)
-
+    to_e(jnp.concatenate([far_c[q] for q in range(4)], axis=0), 4)
     descend(4, w_t2, far_b)
     descend(8, w_t1, far_a)
-
-    def leaf_down(g):
-        for half in range(2):
-            q = 2 * g + half
-            lhs = e_down[pl.ds(4 * q, 4)].reshape(64, 256)
-            value = near_f[q] + pick_diagonal(times([lhs], [half_of(w_lb, g, half)]))
-            for i in range(2):
-                vals[2 * q + i] = value[:, 128 * i : 128 * i + 128]
-
-    each(8, UP_UNROLL, leaf_down)
+    each(8, DOWN_UNROLL, leaf_down)
+
+    over(1, 8, lambda q: d_copy(q).wait_recv())
+    falling = e_rows(unpack(total_of(d_buf, 8)))
+    for q in range(16):
+        value = near_f[q] + dot(falling, z_w[q])
+        for i in range(2):
+            vals[2 * q + i] = value[:, 128 * i : 128 * i + 128]
 
     up_copy.wait_send()
     down_copy.wait_send()
@@ -567,6 +613,9 @@
         vm((38, 16, 256), BF16),
         vm((22, 16, 256), BF16),
         vm((64, 16, 256), BF16),
+        vm((16, 64, 256), F32),
+        vm((64, 64, 256), BF16),
+        vm((16, 256, 256), BF16),
         vm((16, 16, 256), F32),
         vm((16, 16, 256), F32),
         vm((8, 16, 256), F32),

time: 42.3 us -> 41.5 us (0.981)
  Pallas kernels: 42.1 us -> 41.2 us
    pallas_call x1, Pallas kernels: 39 us -> 38.1 us  [body(): pl.pallas_call(functools.partial(kernel, devices), out_shape=(jax.ShapeDt...]
where the time goes in v5:
time: 41.5 us; the launch traced here: 41.2 us
  Pallas kernels  41.2 us (99%)
    pallas_call x1, Pallas kernels, body(): pl.pallas_call(functools.partial(kernel, devices), out_shape=(jax.ShapeDt...  38.1 us
    pallas_call x1, Pallas kernels, body(): pl.pallas_call(restore, out_shape=jax.ShapeDtypeStruct((16, 4096), F32),...  3.07 us

profile of v5, /device:TPU:1, one launch (start us, length us, event | category | flops | bytes accessed | tf_op | source)
XLA Modules:
  0.0 41.2 jit_solution(11163983413750884111)
XLA Ops:
  0.0 38.1 %shard_map.172 = (f32[32,16,128]{2,1,0:T(8,128)}, s32[64,128]{1,0:T(8,128)}) custom-call(f32[16,4096]{1,0:T(8,128)} %rhs_h.1, s32[1,4096]{1,0:T(1,128)} %order_h.1, f32[2048,128]{1,0:T(8,128)} %bitcast.49, s32[3,64]{1,0:T(4,128)} %near_pick.1, f32[3,2048,128]{2,1,0:T(8,128)} %bitcast.46, f32[2048,128]{1,0:T(8,128)} %bitcast.50, f32[1024,128]{1,0:T(8,128)} %bitcast.52, ...), custom_call_target="tpu_custom_call" | custom-call | tf_op jit(solution)/shard_map/pallas_call | solution.py:646
  38.1 3.1 %shard_map.173 = f32[16,4096]{1,0:T(8,128)} custom-call(f32[32,16,128]{2,1,0:T(8,128)} %get-tuple-element.7.vals, s32[64,128]{1,0:T(8,128)} %get-tuple-element.8.inverse), custom_call_target="tpu_custom_call" | custom-call | tf_op jit(solution)/shard_map/pallas_call | solution.py:659

commit v6 on v5

--- a/solution.py
+++ b/solution.py
@@ -140,7 +140,7 @@
     w_lb, w_t1, w_t2, w_tr, to_d, to_n, diagonal, dmat, table, tiles,
     e_ord, e0, e1, e2, e_down, z_d, z_e, z_w, near_f, far_a, far_b, far_c,
     halo_up, halo_down, from_below, from_above,
-    a_send, a_buf, b_send, b_buf, c_send, c_buf, d_send, d_buf,
+    a_send, a_buf, b_send, b_buf, c_send, c_other, c_sum, c_buf, d_send, d_buf,
     load_sem, halo_sems, a_ssem, a_rsem, b_ssem, b_rsem, c_ssem, c_rsem, d_ssem, d_rsem,
 ):
     me = lax.axis_index("leaf")
@@ -152,23 +152,38 @@
     wide = count // deep
     line, depth = group // deep, group & (deep - 1)
 
-    def hops(offset):
-        dx, dz = offset
+    core, sibling = me & 1, me ^ 1
+    share, turns = count // 2, max(deep // 2, 1)
+
+    def offset(m, parity):
+        dx = m // turns
+        return dx, 2 * (m % turns) + ((parity ^ dx) & 1)
+
+    def hops(m):
+        dx, dz = offset(m, 0)
         return min(dx, wide - dx) + min(dz, deep - dz)
 
-    offsets = sorted(((dx, dz) for dx in range(wide) for dz in range(deep)), key=hops)[::-1]
-    offsets = [(0, 0)] + offsets[:-1]
-
-    def group_at(q, sign=1):
-        dx, dz = offsets[q]
-        dx, dz = (dx, dz) if sign > 0 else (wide - dx, deep - dz)
+    order_of_turns = sorted(range(1, share), key=hops)[::-1]
+
+    def group_at(m, parity):
+        dx, dz = offset(m, parity)
         return ((line + dx) & (wide - 1)) * deep + ((depth + dz) & (deep - 1))
+
+    def slot_of(node):
+        dx = (line - (node >> (deep.bit_length() - 1))) & (wide - 1)
+        dz = (depth - (node & (deep - 1))) & (deep - 1)
+        return ((dx + dz) & 1) * share + dx * turns + (dz >> 1)
 
     def mate(q):
         return base + ((inside + q) & 7)
 
     def far_mate(q):
-        return group_at(q) * 8 + inside
+        return group_at(q, core) * 8 + inside
+
+    def each_turn(action):
+        for m in order_of_turns:
+            action(m)
+        pl.when(core == 1)(lambda: action(0))
 
     loads = {}
 
@@ -192,8 +207,7 @@
     def _(q):
         greet(mate(q))
 
-    for q in range(1, count):
-        greet(far_mate(q))
+    each_turn(lambda m: greet(far_mate(m)))
 
     rows, lanes = iota((256, 256), 0), iota((256, 256), 1)
 
@@ -335,7 +349,7 @@
     a_send[...] = offered
     a_buf[0] = offered
 
-    pl.semaphore_wait(barrier, 2 + 7 + count - 1)
+    pl.semaphore_wait(barrier, 2 + 7 + share - 1 + core)
 
     def remote(src, dst, send, receive, device):
         return pltpu.make_async_remote_copy(
@@ -346,15 +360,17 @@
     def a_copy(q):
         return remote(a_send, a_buf.at[q], a_ssem.at[q], a_rsem.at[q], mate(q))
 
-    def b_copy(q):
-        return remote(b_send, b_buf.at[group], b_ssem.at[q], b_rsem.at[group], far_mate(q))
-
-    def b_arrival(q):
-        origin = group_at(q, -1)
-        return remote(b_send, b_buf.at[origin], b_ssem.at[q], b_rsem.at[origin], far_mate(q))
-
-    def c_copy(q):
-        return remote(c_send.at[q], c_buf.at[q], c_ssem.at[q], c_rsem.at[q], far_mate(q))
+    def b_copy(m):
+        at = core * share + m
+        return remote(b_send, b_buf.at[at], b_ssem.at[m], b_rsem.at[m], far_mate(m))
+
+    half_here = pl.ds(core * share, share)
+    half_there = pl.ds((1 - core) * share, share)
+    b_half = remote(b_buf.at[half_here], b_buf.at[half_here], halo_sems.at[4], halo_sems.at[5], sibling)
+    c_half = remote(c_send.at[half_there], c_other, halo_sems.at[6], halo_sems.at[7], sibling)
+
+    def c_copy(m):
+        return remote(c_sum.at[m], c_buf.at[m], c_ssem.at[m], c_rsem.at[m], far_mate(m))
 
     def d_copy(q):
         return remote(d_send, d_buf.at[q], d_ssem.at[q], d_rsem.at[q], mate(q))
@@ -505,8 +521,12 @@
 
     summed = total_of(a_buf, 8)
     b_send[...] = summed
-    b_buf[group] = summed
-    over(1, count, lambda q: b_copy(q).start())
+
+    @pl.when(core == 0)
+    def _():
+        b_buf[0] = summed
+
+    each_turn(lambda m: b_copy(m).start())
 
     compose(8, w_t1)
     loads["near"].wait()
@@ -515,27 +535,36 @@
     loads["tb"].wait()
     w_top = split_rows([tb_v[pl.ds(n, 32, stride=4), :] for n in range(4)])
 
-    over(1, count, lambda q: b_arrival(q).wait_recv())
+    each_turn(lambda m: b_copy(m).wait_recv())
+    b_half.start()
+    b_half.wait_recv()
 
     picked = []
     for b in range(4):
-        picked.append(e_rows(unpack(b_buf[top_source[b]])))
+        picked.append(e_rows(unpack(b_buf[slot_of(top_source[b])])))
     coupled = pick_diagonal(times([jnp.concatenate(picked, axis=0)], [w_top]))
     moved = dot(jnp.concatenate(split(coupled), axis=0), to_n[...])
     moved = moved[0:16] + moved[16:32]
     packed = []
     for i in range(2):
         packed += [pack(block) for block in pair(moved[:, 128 * i : 128 * i + 128])]
-    for q in range(count):
-        target = group_at(q)
-        part = jnp.zeros((8, 128), F32)
-        for b in range(4):
-            part = part + jnp.where(jnp.full((8, 128), top_target[b]) == target, packed[b], 0.0)
-        if q == 0:
-            c_buf[0] = part
-        else:
-            c_send[q] = part
-    over(1, count, lambda q: c_copy(q).start())
+    for parity in range(2):
+        for m in range(share):
+            target = group_at(m, parity)
+            part = jnp.zeros((8, 128), F32)
+            for b in range(4):
+                part = part + jnp.where(jnp.full((8, 128), top_target[b]) == target, packed[b], 0.0)
+            c_send[parity * share + m] = part
+    c_half.start()
+    c_half.wait_recv()
+    for m in range(share):
+        c_sum[m] = c_send[core * share + m] + c_other[m]
+
+    @pl.when(core == 0)
+    def _():
+        c_buf[0] = c_sum[0]
+
+    each_turn(lambda m: c_copy(m).start())
 
     compose_leaves()
     loads["fc"].wait()
@@ -545,8 +574,8 @@
     loads["fa"].wait()
     each(8, NEAR_UNROLL, lambda g: partners(g, pick_a, fa_v, e0, far_shift, far_a))
 
-    over(1, count, lambda q: c_copy(q).wait_recv())
-    summed = total_of(c_buf, count)
+    each_turn(lambda m: c_copy(m).wait_recv())
+    summed = total_of(c_buf, share)
     d_send[...] = summed
     d_buf[0] = summed
     over(1, 8, lambda q: d_copy(q).start())
@@ -566,8 +595,10 @@
     up_copy.wait_send()
     down_copy.wait_send()
     over(1, 8, lambda q: a_copy(q).wait_send())
-    over(1, count, lambda q: b_copy(q).wait_send())
-    over(1, count, lambda q: c_copy(q).wait_send())
+    b_half.wait_send()
+    c_half.wait_send()
+    each_turn(lambda m: b_copy(m).wait_send())
+    each_turn(lambda m: c_copy(m).wait_send())
     over(1, 8, lambda q: d_copy(q).wait_send())
 
 
@@ -629,17 +660,19 @@
         vm((8, 128), F32),
         vm((count, 8, 128), F32),
         vm((count, 8, 128), F32),
-        vm((count, 8, 128), F32),
+        vm((count // 2, 8, 128), F32),
+        vm((count // 2, 8, 128), F32),
+        vm((count // 2, 8, 128), F32),
         vm((8, 128), F32),
         vm((8, 8, 128), F32),
         dma((12,)),
-        dma((4,)),
         dma((8,)),
         dma((8,)),
-        dma((count,)),
-        dma((count,)),
-        dma((count,)),
-        dma((count,)),
+        dma((8,)),
+        dma((count // 2,)),
+        dma((count // 2,)),
+        dma((count // 2,)),
+        dma((count // 2,)),
         dma((8,)),
         dma((8,)),
     ]

time: 41.5 us -> 42.8 us (1.031)
  Pallas kernels: 41.2 us -> 42.5 us
    pallas_call x1, Pallas kernels: 38.1 us -> 39.5 us  [body(): pl.pallas_call(functools.partial(kernel, devices), out_shape=(jax.ShapeDt...]
where the time goes in v6:
time: 42.8 us; the launch traced here: 42.5 us
  Pallas kernels  42.5 us (99%)
    pallas_call x1, Pallas kernels, body(): pl.pallas_call(functools.partial(kernel, devices), out_shape=(jax.ShapeDt...  39.5 us
    pallas_call x1, Pallas kernels, body(): pl.pallas_call(restore, out_shape=jax.ShapeDtypeStruct((16, 4096), F32),...  3.06 us

profile of v6, /device:TPU:1, one launch (start us, length us, event | category | flops | bytes accessed | tf_op | source)
XLA Modules:
  0.0 42.5 jit_solution(12948741796628942786)
XLA Ops:
  0.0 39.5 %shard_map.172 = (f32[32,16,128]{2,1,0:T(8,128)}, s32[64,128]{1,0:T(8,128)}) custom-call(f32[16,4096]{1,0:T(8,128)} %rhs_h.1, s32[1,4096]{1,0:T(1,128)} %order_h.1, f32[2048,128]{1,0:T(8,128)} %bitcast.49, s32[3,64]{1,0:T(4,128)} %near_pick.1, f32[3,2048,128]{2,1,0:T(8,128)} %bitcast.46, f32[2048,128]{1,0:T(8,128)} %bitcast.50, f32[1024,128]{1,0:T(8,128)} %bitcast.52, ...), custom_call_target="tpu_custom_call" | custom-call | tf_op jit(solution)/shard_map/pallas_call | solution.py:679
  39.5 3.1 %shard_map.173 = f32[16,4096]{1,0:T(8,128)} custom-call(f32[32,16,128]{2,1,0:T(8,128)} %get-tuple-element.7.vals, s32[64,128]{1,0:T(8,128)} %get-tuple-element.8.inverse), custom_call_target="tpu_custom_call" | custom-call | tf_op jit(solution)/shard_map/pallas_call | solution.py:692

commit v7 on v5

--- a/solution.py
+++ b/solution.py
@@ -492,9 +492,6 @@
             lhs = e_down[pl.ds(4 * q, 4)].reshape(64, 256)
             near_f[q] = near_f[q] + pick_diagonal(times([lhs], [half_of(w_lb, g, half)]))
 
-    compose_two()
-    compose(4, w_t2)
-
     over(1, 8, lambda q: a_copy(q).wait_recv())
 
     def total_of(buffer, slots):
@@ -508,10 +505,10 @@
     b_buf[group] = summed
     over(1, count, lambda q: b_copy(q).start())
 
+    compose_two()
+    compose(4, w_t2)
     compose(8, w_t1)
     loads["near"].wait()
-    near_part(0)
-    near_part(4)
     loads["tb"].wait()
     w_top = split_rows([tb_v[pl.ds(n, 32, stride=4), :] for n in range(4)])
 
@@ -537,6 +534,8 @@
             c_send[q] = part
     over(1, count, lambda q: c_copy(q).start())
 
+    near_part(0)
+    near_part(4)
     compose_leaves()
     loads["fc"].wait()
     each(2, NEAR_UNROLL, lambda g: partners(g, pick_c, fc_v, e2, far_shift, far_c))

time: 41.5 us -> 41.6 us (level)
  no operation moved by 1% of the time
where the time goes in v7:
time: 41.6 us; the launch traced here: 41.5 us
  Pallas kernels  41.5 us (100%)
    pallas_call x1, Pallas kernels, body(): pl.pallas_call(functools.partial(kernel, devices), out_shape=(jax.ShapeDt...  38.4 us
    pallas_call x1, Pallas kernels, body(): pl.pallas_call(restore, out_shape=jax.ShapeDtypeStruct((16, 4096), F32),...  3.06 us

profile of v7, /device:TPU:1, one launch (start us, length us, event | category | flops | bytes accessed | tf_op | source)
XLA Modules:
  0.0 41.5 jit_solution(17038651290025762340)
XLA Ops:
  0.0 38.4 %shard_map.172 = (f32[32,16,128]{2,1,0:T(8,128)}, s32[64,128]{1,0:T(8,128)}) custom-call(f32[16,4096]{1,0:T(8,128)} %rhs_h.1, s32[1,4096]{1,0:T(1,128)} %order_h.1, f32[2048,128]{1,0:T(8,128)} %bitcast.49, s32[3,64]{1,0:T(4,128)} %near_pick.1, f32[3,2048,128]{2,1,0:T(8,128)} %bitcast.46, f32[2048,128]{1,0:T(8,128)} %bitcast.50, f32[1024,128]{1,0:T(8,128)} %bitcast.52, ...), custom_call_target="tpu_custom_call" | custom-call | tf_op jit(solution)/shard_map/pallas_call | solution.py:645
  38.4 3.1 %shard_map.173 = f32[16,4096]{1,0:T(8,128)} custom-call(f32[32,16,128]{2,1,0:T(8,128)} %get-tuple-element.7.vals, s32[64,128]{1,0:T(8,128)} %get-tuple-element.8.inverse), custom_call_target="tpu_custom_call" | custom-call | tf_op jit(solution)/shard_map/pallas_call | solution.py:658
